TPU v7x, 32 devices: a whole 2x2x4 slice. The times are simulated.
32 devices in a mesh: groups: 2 (over y), gz: 4 (over x, core), xy: 4 (over z).
Axes of the slice: x: 2, y: 2, z: 4, core: 2. Of those that a mesh axis runs over, the one named last changes fastest.
Arguments:
- features: bfloat16 [16, 32, 32, 128], P(('groups', 'gz'), 'xy'), parts along dimension 0, may hold values from -6 to 6
- species: int32 [16, 32, 32], P(('groups', 'gz'), 'xy'), parts along dimension 0, may hold values from 0 to 7
- sublayer: int32 [16, 32, 32], P(('groups', 'gz'), 'xy'), parts along dimension 0, may hold values from 0 to 1
- offsets: float32 [2, 16, 32, 32], P(None, ('groups', 'gz'), 'xy'), parts along dimension 1, may hold values from 0 to 11
- neighbours: int32 [16, 32, 32, 32], P(('groups', 'gz'), 'xy'), parts along dimension 0, may hold values from 0 to 287
- neighbour_count: int32 [16, 32, 32], P(('groups', 'gz'), 'xy'), parts along dimension 0, may hold values from 16 to 32
- distances: float32 [16, 32, 32, 32], P(('groups', 'gz'), 'xy'), parts along dimension 0, may hold values from 0.8 to 7.8
- species_table: bfloat16 [8, 128], replicated, may hold values from -3 to 3
- charge_weight: bfloat16 [128, 16], replicated, may hold values from -0.5 to 0.5
- radial_in: bfloat16 [8, 64], replicated, may hold values from -2 to 2
- radial_out: bfloat16 [64, 128], replicated, may hold values from -0.75 to 0.75
- update_in: bfloat16 [128, 256], replicated, may hold values from -0.5 to 0.5
- update_out: bfloat16 [256, 128], replicated, may hold values from -0.375 to 0.375
- energy_weight: bfloat16 [128], replicated, may hold values from -0.5 to 0.5
Outputs:
- features_out: bfloat16 [16, 32, 32, 128], P(('groups', 'gz'), 'xy'), parts along dimension 0
- energy: float32 [16, 32, 32], P(('groups', 'gz'), 'xy'), parts along dimension 0
- forces: float32 [2, 16, 32, 32], P(None, ('groups', 'gz'), 'xy'), parts along dimension 1
There are 2 independent parts, one for each index of `groups`. A program takes and returns all parts, laid end to end along the dimension named above; an argument that names none is the same for every part. Nothing has to cross between parts.
Inputs may be any that keep to these rules, and one draw needn't show every extreme that they name: `neighbours`: an entry n names the neighbour at cell offset o = n // 32 (z offset o // 3 - 1, x offset o % 3 - 1) and slot n % 32 of that cell. `neighbour_count`: entries of a list from this count on are padding.
All inputs are finite; a program needn't handle non-finite values.
Results may differ from a plain program's by a relative error of at most 0.0012.
The roundings to bfloat16 on the way count: a program that leaves them out, or rounds other values in their place, can miss the bound.
Values may be sent and summed in bfloat16 or wider, within the bound.
A program may use at most 64 MiB of HBM per device.

v0:
```python
import math

import jax
import jax.numpy as jnp
from jax import lax
from jax.sharding import PartitionSpec as P

KX = 128
KY = 8


cell_width = 11.0
layer_depth = 5.5
screening = 0.025
smearing = 1.0
coupling = 0.25
cutoff = 8.0
basis_width = 1.0


def carried_in(part, axis, combine, identity, reverse):
    count = lax.axis_size(axis)
    place = lax.axis_index(axis)
    ahead = count - 1 - place if reverse else place
    gathered = jax.tree.map(lambda a: lax.all_gather(a, axis), part)
    state = jax.tree.map(lambda a, e: jnp.zeros_like(a) + jnp.asarray(e, a.dtype), part, identity)

    def one(turn, state):
        source = count - 1 - turn if reverse else turn
        return combine(
            state, jax.tree.map(lambda a: lax.dynamic_index_in_dim(a, source, 0, False), gathered)
        )

    return lax.fori_loop(0, ahead, one, state)


def with_halo(cells, sides, width, closed):
    for axis, dim in sides:
        count = lax.axis_size(axis)
        ends = count if closed else count - 1
        head = lax.slice_in_dim(cells, 0, width, axis=dim)
        tail = lax.slice_in_dim(cells, cells.shape[dim] - width, cells.shape[dim], axis=dim)
        cells = jnp.concatenate(
            [
                lax.ppermute(tail, axis, [(i, (i + 1) % count) for i in range(ends)]),
                cells,
                lax.ppermute(head, axis, [((i + 1) % count, i) for i in range(ends)]),
            ],
            axis=dim,
        )
    return cells


def wave_numbers(wave_index, width_x):
    wave_x = 2.0 * math.pi / width_x * (wave_index // KY - KX // 2).astype(jnp.float32)
    wave_y = 2.0 * math.pi / cell_width * (wave_index % KY - KY // 2).astype(jnp.float32)
    return (wave_x, wave_y)


def wave_factors(wave_x, wave_y, width_x):
    square = wave_x * wave_x + wave_y * wave_y
    screened = jnp.sqrt(square + screening * screening)
    weight = (
        coupling
        * (2.0 * math.pi / (width_x * cell_width))
        * jnp.exp(-0.5 * smearing * smearing * square)
        / screened
    )
    return (screened, weight)


def build_panel(layer_field, wave_x, wave_y, weight):
    cosine = layer_field[:, :, 0] * weight
    sin_part = layer_field[:, :, 1] * weight
    cos_rows = jnp.stack([cosine, wave_x * sin_part, wave_y * sin_part], axis=1)
    sin_rows = jnp.stack([sin_part, -wave_x * cosine, -wave_y * cosine], axis=1)
    field_panel = jnp.stack([cos_rows, sin_rows], axis=3)
    shape = field_panel.shape
    return field_panel.reshape(shape[0], 3 * shape[2], 2, shape[4]).astype(jnp.bfloat16)


def phase_table(coord_x, coord_y, wave_x, wave_y):
    angles = coord_x[..., None] * wave_x + coord_y[..., None] * wave_y
    return jnp.concatenate([jnp.cos(angles), jnp.sin(angles)], axis=-1).astype(jnp.bfloat16)


def combine_sums(earlier, following):
    return (earlier[0] * following[1] + following[0], earlier[1] * following[1])


def layer_panel(moments, first_wave, width_x):
    layers = moments.shape[0]
    wave_count = moments.shape[3]
    wave_index = first_wave + jnp.arange(wave_count, dtype=jnp.int32)
    wave_x, wave_y = wave_numbers(wave_index, width_x)
    screened, weight = wave_factors(wave_x, wave_y, width_x)
    layer_steps = jnp.arange(layers, dtype=jnp.int32)
    layer_gap = jnp.abs(layer_steps[:, None] - layer_steps[None, :]).astype(jnp.float32)
    within = jnp.exp(-screened * layer_depth * layer_gap[:, :, None])
    local_field = jnp.einsum("jmk,mcpk->jcpk", within, moments, precision=lax.Precision.HIGHEST)
    top_sum = local_field[layers - 1]
    bottom_sum = local_field[0]
    span_decay = jnp.exp(-screened * layer_depth * layers)
    identity_pair = (jnp.zeros_like(top_sum), jnp.ones_like(span_decay))
    from_below = carried_in((top_sum, span_decay), "gz", combine_sums, identity_pair, False)[0]
    from_above = carried_in((bottom_sum, span_decay), "gz", combine_sums, identity_pair, True)[0]
    rise_steps = (layer_steps + 1).astype(jnp.float32)
    fall_steps = (layers - layer_steps).astype(jnp.float32)
    rise_factor = jnp.exp(-screened * layer_depth * rise_steps[:, None])[:, None, None, :]
    fall_factor = jnp.exp(-screened * layer_depth * fall_steps[:, None])[:, None, None, :]
    layer_field = local_field + rise_factor * from_below + fall_factor * from_above
    return build_panel(layer_field, wave_x, wave_y, weight)


def edge_messages(gathered, spacing, usable, radial_in, radial_out):
    basis_count = radial_in.shape[0]
    centers = (
        cutoff * jnp.arange(basis_count, dtype=jnp.int32).astype(jnp.float32) / (basis_count - 1)
    )
    radial_basis = jnp.exp(-jnp.square((spacing[..., None] - centers) / basis_width)).astype(
        jnp.bfloat16
    )
    filter_hidden = jax.nn.silu(
        jnp.einsum("xsnb,bh->xsnh", radial_basis, radial_in, preferred_element_type=jnp.float32)
    ).astype(jnp.bfloat16)
    filters = jnp.einsum(
        "xsnh,hf->xsnf", filter_hidden, radial_out, preferred_element_type=jnp.float32
    )
    envelope = jnp.square(1.0 - jnp.square(spacing / cutoff))
    edge_weight = jnp.where(usable, envelope, 0.0)
    return jnp.sum(edge_weight[..., None] * filters * gathered.astype(jnp.float32), axis=2).astype(
        jnp.bfloat16
    )


def shards(
    features,
    species,
    sublayer,
    offsets,
    neighbours,
    neighbour_count,
    distances,
    species_table,
    charge_weight,
    radial_in,
    radial_out,
    update_in,
    update_out,
    energy_weight,
):
    zcells, xcells, slot_count, feature_width = features.shape
    channels = charge_weight.shape[1]
    kind_count = species_table.shape[0]
    atoms_row = xcells * slot_count
    wave_count = KX * KY
    onehot = (species[..., None] == jnp.arange(kind_count, dtype=jnp.int32)).astype(jnp.bfloat16)
    embedded = jnp.einsum(
        "zxsk,kf->zxsf", onehot, species_table, preferred_element_type=jnp.float32
    )
    hidden_start = (features.astype(jnp.float32) + embedded).astype(jnp.bfloat16)
    charges = jnp.einsum(
        "zxsf,fc->zxsc", hidden_start, charge_weight, preferred_element_type=jnp.float32
    ).astype(jnp.bfloat16)
    ghost_rows = with_halo(hidden_start, (("gz", 0),), 1, False)
    extended = with_halo(ghost_rows, (("xy", 1),), 1, True)
    xy_index = lax.axis_index("xy")
    width_x = cell_width * (xcells * lax.axis_size("xy"))
    wave_x, wave_y = wave_numbers(jnp.arange(wave_count, dtype=jnp.int32), width_x)
    cell_x = (xy_index * xcells + jnp.arange(xcells, dtype=jnp.int32)).astype(jnp.float32)
    coord_x = cell_width * cell_x[None, :, None] + offsets[0]
    phases = phase_table(
        coord_x.reshape(zcells, atoms_row), offsets[1].reshape(zcells, atoms_row), wave_x, wave_y
    )
    layer_mask = (sublayer[..., None] == jnp.arange(2, dtype=jnp.int32)).astype(jnp.bfloat16)
    weighted = (layer_mask[..., :, None] * charges[..., None, :]).reshape(
        zcells, atoms_row, 2 * channels
    )
    raw_moments = jnp.einsum("zrp,zrk->zpk", weighted, phases, preferred_element_type=jnp.float32)
    moments = raw_moments.reshape(2 * zcells, channels, 2, wave_count)
    phase_blocks = phases.reshape(zcells, atoms_row, 2, wave_count)
    shared_sums = lax.psum_scatter(moments, "xy", scatter_dimension=3, tiled=True)
    panel_part = layer_panel(shared_sums, xy_index * shared_sums.shape[3], width_x)
    shard_piece = lax.all_gather(panel_part, "xy", axis=3, tiled=True)
    pairs = shard_piece.reshape(zcells, 6 * channels, 2, shard_piece.shape[3])
    evaluated = jnp.einsum(
        "zrpk,zqpk->zrq", phase_blocks, pairs, preferred_element_type=jnp.float32
    )
    evaluated = evaluated.reshape(zcells, xcells, slot_count, 2, 3, channels)
    chosen = jnp.where(
        (sublayer == 0)[..., None, None], evaluated[..., 0, :, :], evaluated[..., 1, :, :]
    )
    charge_values = charges.astype(jnp.float32)
    long_energy = 0.5 * jnp.sum(charge_values * chosen[..., 0, :], axis=-1)
    forces = -jnp.stack(
        [
            jnp.sum(charge_values * chosen[..., 1, :], axis=-1),
            jnp.sum(charge_values * chosen[..., 2, :], axis=-1),
        ]
    )
    region = extended.reshape(-1, feature_width)
    offset_code = neighbours // slot_count
    slot_code = neighbours % slot_count
    z_range = jnp.arange(zcells, dtype=jnp.int32)[:, None, None, None]
    x_range = jnp.arange(xcells, dtype=jnp.int32)[None, :, None, None]
    row_index = (
        (z_range + offset_code // 3) * (xcells + 2) + x_range + offset_code % 3
    ) * slot_count + slot_code
    own_slot = jnp.arange(slot_count, dtype=jnp.int32)[None, None, :, None]
    listed = jnp.arange(neighbours.shape[3], dtype=jnp.int32)
    usable = (listed < neighbour_count[..., None]) & jnp.logical_not(
        (offset_code == 4) & (slot_code == own_slot)
    )
    aggregates = []
    for z_row in range(zcells):
        gathered = jnp.take(region, row_index[z_row].reshape(-1), axis=0).reshape(
            xcells, slot_count, -1, feature_width
        )
        aggregates.append(
            edge_messages(gathered, distances[z_row], usable[z_row], radial_in, radial_out)
        )
    aggregate = jnp.stack(aggregates)
    update_hidden = jax.nn.silu(
        jnp.einsum("zxsf,fh->zxsh", aggregate, update_in, preferred_element_type=jnp.float32)
    ).astype(jnp.bfloat16)
    renewed = hidden_start.astype(jnp.float32) + jnp.einsum(
        "zxsh,hf->zxsf", update_hidden, update_out, preferred_element_type=jnp.float32
    )
    energy = jnp.sum(renewed * energy_weight.astype(jnp.float32), axis=-1) + long_energy
    return (renewed.astype(jnp.bfloat16), energy, forces)


def solution(mesh):
    in_specs = (
        P(("groups", "gz"), "xy", None, None),
        P(("groups", "gz"), "xy", None),
        P(("groups", "gz"), "xy", None),
        P(None, ("groups", "gz"), "xy", None),
        P(("groups", "gz"), "xy", None, None),
        P(("groups", "gz"), "xy", None),
        P(("groups", "gz"), "xy", None, None),
        P(),
        P(),
        P(),
        P(),
        P(),
        P(),
        P(),
    )
    out_specs = (
        P(("groups", "gz"), "xy", None, None),
        P(("groups", "gz"), "xy", None),
        P(None, ("groups", "gz"), "xy", None),
    )
    return jax.shard_map(shards, mesh=mesh, in_specs=in_specs, out_specs=out_specs, check_vma=False)
```

profile of v0, /device:TPU:0, one launch (start us, length us, event | category | flops | bytes accessed | tf_op | source)
XLA Modules:
  0.0 225.5 jit_solution(5195714684004285989)
XLA Ops:
  7.4 0.7 fusion.110
  8.3 1.2 fusion.15
  9.5 1.0 convolution_convert_fusion
  11.3 8.2 %cosine_convert_fusion = (bf16[2,256,1024]{2,1,0:T(8,128)(2,1)S(1)}, bf16[2,256,1024]{2,1,0:T(8,128)(2,1)S(1)}) fusion(f32[1024]{0:T(1024)S(1)} %get-tuple-element.229, f32[2,256]{1,0:T(2,128)S(1)} %mul.572, f32[1024]{0:T(1024)S(1)} %get-tuple-element.228, f32[2,256]{1,0:T(2,128)S(1)} %broadcast_add_fusion), kind=kLoop, calls=%fused_computation.25 | loop fusion | flops 2621440 | bytes 2109440 | tf_op jit(solution)/shard_map/convert.12
  20.5 3.2 %copy.55 = f32[4,16,2,1024]{1,0,2,3:T(4,128)} copy(f32[4,16,2,1024]{3,2,1,0:T(2,128)S(1)} %reshape.463) | data formatting | bytes 1048576 | tf_op jit(solution)/shard_map/reshape | solution.py:180
  23.8 2.5 %collective-permute-start = (bf16[1,8,32,128]{3,2,1,0:T(8,128)(2,1)S(1)}, bf16[1,8,32,128]{3,2,1,0:T(8,128)(2,1)S(1)}, u32[]{:S(2)}, u32[]{:S(2)}) collective-permute-start(bf16[1,8,32,128]{3,2,1,0:T(8,128)(2,1)S(1)} %get-tuple-element.217), channel_id=1, source_target_pairs={{0,4},{4,8},{8,12},{1,5},{5,9},{9,13},{2,6},{6,10},{10,14},{3,7},{... | collective-permute-start | bytes 196616 | tf_op jit(solution)/shard_map/ppermute | solution.py:45
  26.3 1.3 collective-permute-start.1
  27.7 9.0 %cosine_convert_fusion.1 = (bf16[2,256,1,1024]{3,1,2,0:T(8,128)(2,1)}, bf16[2,256,1,1024]{3,1,2,0:T(8,128)(2,1)}) fusion(f32[1024]{0:T(1024)S(1)} %get-tuple-element.229, f32[2,256]{1,0:T(2,128)S(1)} %mul.572, f32[1024]{0:T(1024)S(1)} %get-tuple-element.228, f32[2,256]{1,0:T(2,128)S(1)} %broadcast_add_fusion), kind=kLoop, calls=%fused_computation.28 | loop fusion | flops 2621440 | bytes 2109440 | tf_op jit(solution)/shard_map/convert.14
  38.1 2.5 %collective-permute-start.2 = (bf16[4,1,32,128]{3,2,1,0:T(8,128)(2,1)S(1)}, bf16[4,1,32,128]{3,2,1,0:T(8,128)(2,1)S(1)}, u32[]{:S(2)}, u32[]{:S(2)}) collective-permute-start(bf16[4,1,32,128]{3,2,1,0:T(8,128)(2,1)S(1)} %get-tuple-element.207), channel_id=1, source_target_pairs={{0,1},{1,2},{2,3},{3,0},{4,5},{5,6},{6,7},{7,4},{8,9},{9,10},{10,1... | collective-permute-start | bytes 98312 | tf_op jit(solution)/shard_map/ppermute | solution.py:45
  40.5 2.1 collective-permute-start.3
  42.6 7.4 %all-gather = f32[4,1,256]{2,1,0:T(1,128)S(1)} all-gather(f32[1,1,256]{2,1,0:T(1,128)S(1)} %exponential_bitcast_fusion), channel_id=1, replica_groups=mesh['groups'=2,'gz'=4,'xy'=4] {'gz'}, dimensions={0}, use_global_device_ids=true | all-gather | bytes 5120 | tf_op jit(solution)/shard_map/all_gather | solution.py:25
  51.4 29.4 %gather_fusion = bf16[8192,128]{1,0:T(8,128)(2,1)} fusion(bf16[1280,128]{1,0:T(8,128)(2,1)S(1)} %bitcast.193, s32[8192]{0:T(1024)S(1)} %fusion.66), kind=kCustom, calls=%fused_computation.clone | custom fusion | bytes 4227072 | tf_op jit(solution)/shard_map/jit(_take)/gather | solution.py:216
  80.8 24.0 %gather_fusion.1 = bf16[8192,128]{1,0:T(8,128)(2,1)S(1)} fusion(bf16[1280,128]{1,0:T(8,128)(2,1)S(1)} %bitcast.194, s32[8192]{0:T(1024)S(1)} %fusion.67), kind=kCustom, calls=%fused_computation.1.clone | custom fusion | bytes 4227072 | tf_op jit(solution)/shard_map/jit(_take)/gather | solution.py:216
  104.8 6.6 %broadcast_select_fusion.1 = bf16[8192,128]{1,0:T(8,128)(2,1)} fusion(bf16[8192,128]{1,0:T(8,128)(2,1)} %gather_fusion, pred[8192]{0:T(1024)(128)(4,1)S(1)} %compare_and_fusion.1), kind=kLoop, calls=%fused_computation.31 | loop fusion | flops 1048576 | bytes 4202496 | tf_op jit(solution)/shard_map/jit(_take)/select_n | solution.py:216
  111.5 5.1 %broadcast_select_fusion = bf16[8192,128]{1,0:T(8,128)(2,1)} fusion(bf16[8192,128]{1,0:T(8,128)(2,1)S(1)} %gather_fusion.1, pred[8192]{0:T(1024)(128)(4,1)S(1)} %compare_and_fusion), kind=kLoop, calls=%fused_computation.30 | loop fusion | flops 1048576 | bytes 4202496 | tf_op jit(solution)/shard_map/jit(_take)/select_n | solution.py:216
  116.5 3.9 %fusion.3 = bf16[8,32,128]{2,1,0:T(8,128)(2,1)S(1)} fusion(bf16[8,32,32,128]{3,2,1,0:T(8,128)(2,1)} %bitcast.196, f32[8,32,32]{2,1,0:T(8,128)S(1)} %get-tuple-element.199, f32[8]{0:T(128)S(1)} %convert_multiply_fusion.8, f32[8,32,32]{2,1,0:T(8,128)S(1)} %get-tuple-element.203, bf16[64,128]{1,0:T(8,128)(2,1)S(1)} %copy-done.9, bf16[8,64]{1,0:T(8,128)(2,1)S(1)} %copy-done.10), kind=kOutput, calls=%fused_computation.13 | convolution fusion | flops 149651456 | bytes 2245664 | tf_op jit(solution)/shard_map/xsnh,hf->xsnf/dot_general | solution.py:126
  120.5 2.2 fusion.2
  122.8 1.1 multiply_reduce_fusion
  123.8 59.1 %all-reduce.3.cloned.1.call-done = f32[4,16,2,1024]{1,0,2,3:T(4,128)} async-done(((f32[4,16,2,1024]{1,0,2,3:T(4,128)}), f32[4,16,2,1024]{1,0,2,3:T(4,128)}) %all-reduce.3.cloned.1.call-update) | async-done | bytes 524304
  182.9 3.4 %fusion.16 = f32[256,16,2,4]{1,3,2,0:T(4,128)S(1)} fusion(f32[4,16,2,1024]{1,0,2,3:T(4,128)} %all-reduce.3.cloned.1.call-done, u32[]{:T(128)S(6)} %multiply.24, f32[4,4]{1,0:T(4,128)S(1)} %abs_convert_fusion, f32[256]{0:T(256)S(1)} %negate_multiply_fusion), kind=kOutput, calls=%fused_computation.37 | convolution fusion | flops 1576960 | bytes 1180740 | tf_op jit(solution)/shard_map/jmk,mcpk->jcpk/dot_general | solution.py:100
  186.7 5.4 %all_gather.17 = f32[4,16,2,256]{3,1,2,0:T(8,128)S(1)} all-gather(f32[1,16,2,256]{3,1,2,0:T(8,128)S(1)} %get-tuple-element.216), channel_id=1, replica_groups=mesh['groups'=2,'gz'=4,'xy'=4] {'gz'}, dimensions={0}, use_global_device_ids=true | all-gather | bytes 163840 | tf_op jit(solution)/shard_map/all_gather | solution.py:25
  192.5 5.6 %all_gather.16 = f32[4,16,2,256]{3,1,2,0:T(8,128)S(1)} all-gather(f32[1,16,2,256]{3,1,2,0:T(8,128)S(1)} %get-tuple-element.215), channel_id=1, replica_groups=mesh['groups'=2,'gz'=4,'xy'=4] {'gz'}, dimensions={0}, use_global_device_ids=true | all-gather | bytes 163840 | tf_op jit(solution)/shard_map/all_gather | solution.py:25
  198.3 17.9 %all_gather.18 = bf16[4,48,2,1024]{3,1,0,2:T(8,128)(2,1)S(1)} all-gather(bf16[4,48,2,256]{3,1,0,2:T(8,128)(2,1)S(1)} %pad_maximum_fusion.1), channel_id=1, replica_groups=mesh['groups'=2,'gz'=4,'xy'=4] {'xy'}, dimensions={3}, use_global_device_ids=true | all-gather | bytes 983040 | tf_op jit(solution)/shard_map/all_gather | solution.py:184
  216.2 0.8 fusion.12
  (101 shorter events, 7.1 us)
Async XLA Ops:
  7.2 115.6 %copy-start = (bf16[256,128]{1,0:T(8,128)(2,1)S(1)}, bf16[256,128]{1,0:T(8,128)(2,1)}, u32[]{:S(2)}) copy-start(bf16[256,128]{1,0:T(8,128)(2,1)} %param.32) | copy-start | bytes 196612
  7.2 175.7 %all-reduce.3.cloned.1.call-start = ((), (), s32[]{:S(2)}) async-start(), calls=%async_computation | async-start | bytes 8388608
  23.7 13.0 %copy-start.6 = (s32[2,8,32]{2,1,0:T(8,128)S(1)}, s32[2,8,32]{2,1,0:T(8,128)}, u32[]{:S(2)}) copy-start(s32[2,8,32]{2,1,0:T(8,128)} %param.22) | copy-start | bytes 6148
  23.7 13.0 %copy-start.4 = (s32[2,8,32,32]{3,2,1,0:T(8,128)S(1)}, s32[2,8,32,32]{3,2,1,0:T(8,128)}, u32[]{:S(2)}) copy-start(s32[2,8,32,32]{3,2,1,0:T(8,128)} %param.24) | copy-start | bytes 196612
  23.7 13.8 %copy-start.7 = (s32[2,8,32]{2,1,0:T(8,128)S(1)}, s32[2,8,32]{2,1,0:T(8,128)}, u32[]{:S(2)}) copy-start(s32[2,8,32]{2,1,0:T(8,128)} %param.25) | copy-start | bytes 6148
  23.7 14.1 %copy-start.5 = (f32[2,8,32,32]{3,2,1,0:T(8,128)S(1)}, f32[2,8,32,32]{3,2,1,0:T(8,128)}, u32[]{:S(2)}) copy-start(f32[2,8,32,32]{3,2,1,0:T(8,128)} %param.26) | copy-start | bytes 196612
  23.8 14.3 %collective-permute-start = (bf16[1,8,32,128]{3,2,1,0:T(8,128)(2,1)S(1)}, bf16[1,8,32,128]{3,2,1,0:T(8,128)(2,1)S(1)}, u32[]{:S(2)}, u32[]{:S(2)}) collective-permute-start(bf16[1,8,32,128]{3,2,1,0:T(8,128)(2,1)S(1)} %get-tuple-element.217), channel_id=1, source_target_pairs={{0,4},{4,8},{8,12},{1,5},{5,9},{9,13},{2,6},{6,10},{10,14},{3,7},{... | collective-permute-start | bytes 196616 | tf_op jit(solution)/shard_map/ppermute | solution.py:45
  26.3 11.8 %collective-permute-start.1 = (bf16[1,8,32,128]{3,2,1,0:T(8,128)(2,1)S(1)}, bf16[1,8,32,128]{3,2,1,0:T(8,128)(2,1)S(1)}, u32[]{:S(2)}, u32[]{:S(2)}) collective-permute-start(bf16[1,8,32,128]{3,2,1,0:T(8,128)(2,1)S(1)} %get-tuple-element.218), channel_id=1, source_target_pairs={{4,0},{8,4},{12,8},{5,1},{9,5},{13,9},{6,2},{10,6},{14,10},{7,3},{... | collective-permute-start | bytes 196616 | tf_op jit(solution)/shard_map/ppermute | solution.py:47
  36.7 13.4 %copy-start.11 = (bf16[128]{0:T(256)(128)(2,1)S(1)}, bf16[128]{0:T(256)(128)(2,1)}, u32[]{:S(2)}) copy-start(bf16[128]{0:T(256)(128)(2,1)} %param.33) | copy-start | bytes 772
  36.7 13.4 %copy-start.12 = (u32[32]{0:T(128)S(1)}, u32[32]{0:T(128)}, u32[]{:S(2)}) copy-start(u32[32]{0:T(128)} %constant.222) | copy-start | bytes 388
  38.1 13.2 %collective-permute-start.2 = (bf16[4,1,32,128]{3,2,1,0:T(8,128)(2,1)S(1)}, bf16[4,1,32,128]{3,2,1,0:T(8,128)(2,1)S(1)}, u32[]{:S(2)}, u32[]{:S(2)}) collective-permute-start(bf16[4,1,32,128]{3,2,1,0:T(8,128)(2,1)S(1)} %get-tuple-element.207), channel_id=1, source_target_pairs={{0,1},{1,2},{2,3},{3,0},{4,5},{5,6},{6,7},{7,4},{8,9},{9,10},{10,1... | collective-permute-start | bytes 98312 | tf_op jit(solution)/shard_map/ppermute | solution.py:45
  40.5 10.7 %collective-permute-start.3 = (bf16[4,1,32,128]{3,2,1,0:T(8,128)(2,1)S(1)}, bf16[4,1,32,128]{3,2,1,0:T(8,128)(2,1)S(1)}, u32[]{:S(2)}, u32[]{:S(2)}) collective-permute-start(bf16[4,1,32,128]{3,2,1,0:T(8,128)(2,1)S(1)} %get-tuple-element.208), channel_id=1, source_target_pairs={{1,0},{2,1},{3,2},{0,3},{5,4},{6,5},{7,6},{4,7},{9,8},{10,9},{11,1... | collective-permute-start | bytes 98312 | tf_op jit(solution)/shard_map/ppermute | solution.py:47
  111.4 5.1 %copy-start.9 = (bf16[64,128]{1,0:T(8,128)(2,1)S(1)}, bf16[64,128]{1,0:T(8,128)(2,1)}, u32[]{:S(2)}) copy-start(bf16[64,128]{1,0:T(8,128)(2,1)} %param.30) | copy-start | bytes 49156
  111.5 5.1 %copy-start.10 = (bf16[8,64]{1,0:T(8,128)(2,1)S(1)}, bf16[8,64]{1,0:T(8,128)(2,1)}, u32[]{:S(2)}) copy-start(bf16[8,64]{1,0:T(8,128)(2,1)} %param.29) | copy-start | bytes 3076
  116.5 4.0 %copy-start.1 = (bf16[8192,128]{1,0:T(8,128)(2,1)S(1)}, bf16[8192,128]{1,0:T(8,128)(2,1)}, u32[]{:S(2)}) copy-start(bf16[8192,128]{1,0:T(8,128)(2,1)} %broadcast_select_fusion) | copy-start | bytes 6291460
  120.5 2.3 %copy-start.8 = (bf16[128,256]{1,0:T(8,128)(2,1)S(1)}, bf16[128,256]{1,0:T(8,128)(2,1)}, u32[]{:S(2)}) copy-start(bf16[128,256]{1,0:T(8,128)(2,1)} %param.31) | copy-start | bytes 196612
  192.5 23.7 %copy-start.2 = (bf16[2,256,1,1024]{3,1,2,0:T(8,128)(2,1)S(1)}, bf16[2,256,1,1024]{3,1,2,0:T(8,128)(2,1)}, u32[]{:S(2)}) copy-start(bf16[2,256,1,1024]{3,1,2,0:T(8,128)(2,1)} %get-tuple-element.223) | copy-start | bytes 3145732
  192.5 23.6 %copy-start.3 = (bf16[2,256,1,1024]{3,1,2,0:T(8,128)(2,1)S(1)}, bf16[2,256,1,1024]{3,1,2,0:T(8,128)(2,1)}, u32[]{:S(2)}) copy-start(bf16[2,256,1,1024]{3,1,2,0:T(8,128)(2,1)} %get-tuple-element.224) | copy-start | bytes 3145732
Sparse Core Ops, SparseCore 0:
  23.8 159.0 all-reduce.2
where the time goes:
time: 226 us
  local copies, waits for them, and re-layouts  60 us (27%)
  waiting for transfers between devices  59.1 us (26%)
  blocking collectives  36.2 us (16%)
  other arithmetic  32.5 us (14%)
  between operations  15.2 us (7%)
  matrix products  14 us (6%)
  starting transfers between devices  8.37 us (4%)
    unnamed x2, waiting for transfers between devices  59.1 us
    gather x2, local copies, waits for them, and re-layouts, shards(): jnp.take(region, row_index[z_row].reshape(-1), axis=0)  53.5 us
    all_gather x3, blocking collectives, carried_in(): gathered = jax.tree.map(lambda a: lax.all_gather(a, axis), part)  18.4 us
    all_gather x1, blocking collectives, shards(): shard_piece = lax.all_gather(panel_part, 'xy', axis=3, tiled=True)  17.9 us
    another operation x4, other arithmetic  17.2 us
    select_n x2, other arithmetic, shards(): jnp.take(region, row_index[z_row].reshape(-1), axis=0)  11.7 us
    dot_general x2, matrix products, edge_messages(): jnp.einsum('xsnh,hf->xsnf', filter_hidden, radial_out, preferred_element_...  6.18 us
    ppermute x2, starting transfers between devices, with_halo(): lax.ppermute(tail, axis, [(i, (i + 1) % count) for i in range(ends)])  4.95 us
  transfers between devices with their start and end apart: 5, of which 1 were waited for; matrix products, arithmetic and copies ran while one was open for 37% of the time, Pallas kernels for 0%

commit v1 on v0

v1 whole, which is shorter than its diff:
```python
import functools
import math

import jax
import jax.numpy as jnp
import numpy as np
from jax import lax
from jax.experimental import pallas as pl
from jax.experimental.pallas import tpu as pltpu
from jax.sharding import PartitionSpec as P

KX = 128
KY = 8
MESH = pl.DeviceIdType.MESH

cell_width = 11.0
layer_depth = 5.5
screening = 0.025
smearing = 1.0
coupling = 0.25
cutoff = 8.0

BLOCKS = (4, 0, 5, 6, 7)
WAVES = KX * len(BLOCKS)


def wave_constants(width_x, layers):
    index_x = np.tile(np.arange(KX), len(BLOCKS))
    index_y = np.repeat(np.array(BLOCKS), KX)
    count = np.ones(WAVES, np.float32)
    count[2 * KX :][index_x[2 * KX :] > 0] = 2.0
    count[1 : KX // 2] = 2.0
    count[KX // 2 + 1 : KX] = 0.0
    for spare, j in enumerate((1, 2, 3)):
        index_x[KX // 2 + 1 + spare] = 0
        index_y[KX // 2 + 1 + spare] = j
        count[KX // 2 + 1 + spare] = 1.0
    f32 = np.float32
    wave_x = f32(2.0 * math.pi / width_x) * (index_x - KX // 2).astype(f32)
    wave_y = f32(2.0 * math.pi / cell_width) * (index_y - KY // 2).astype(f32)
    square = wave_x * wave_x + wave_y * wave_y
    screened = np.sqrt(square + f32(screening * screening))
    weight = f32(coupling * (2.0 * math.pi / (width_x * cell_width))) * np.exp(
        f32(-0.5 * smearing * smearing) * square
    )
    weight = weight / screened * count
    row_x = np.zeros(WAVES, f32)
    row_x[:KX] = f32(2.0 * math.pi / width_x) * (np.arange(KX) - KX // 2).astype(f32)
    row_y = np.zeros(WAVES, f32)
    row_y[: len(BLOCKS) - 1] = f32(2.0 * math.pi / cell_width) * (
        np.array(BLOCKS[1:]) - KY // 2
    ).astype(f32)
    powers = [np.exp(-screened * f32(layer_depth) * f32(n)) for n in range(layers + 1)]
    rows = [wave_x, wave_y, weight, row_x, row_y] + powers
    rows += [np.zeros(WAVES, f32)] * (-len(rows) % 8)
    return np.stack(rows).astype(f32)


def sincos(angle):
    turns = jnp.floor(angle * (2.0 / math.pi) + 0.5)
    rest = angle - turns * 1.5703125
    rest = rest - turns * 4.8375129699707031e-4
    rest = rest - turns * 7.5497899548918822e-8
    square = rest * rest
    sine = rest + rest * square * (
        (-1.9515295891e-4 * square + 8.3321608736e-3) * square - 1.6666654611e-1
    )
    cosine = (1.0 - 0.5 * square) + square * square * (
        (2.443315711809948e-5 * square - 1.388731625493765e-3) * square + 4.166664568298827e-2
    )
    quadrant = turns.astype(jnp.int32)
    swap = (quadrant & 1) == 1
    out_sin = jnp.where(swap, cosine, sine)
    out_cos = jnp.where(swap, sine, cosine)
    out_sin = jnp.where((quadrant & 2) == 2, -out_sin, out_sin)
    out_cos = jnp.where(((quadrant + 1) & 2) == 2, -out_cos, out_cos)
    return out_sin, out_cos


def silu(value):
    half = 0.5 * value
    return half + half * jnp.tanh(half)


def dot(a, b):
    return jnp.dot(a, b, preferred_element_type=jnp.float32)


def kernel(
    sizes,
    feat,
    atom_rows,
    near,
    dist,
    table,
    charge_cols,
    hidden_in,
    hidden_out,
    update_in,
    update_out,
    energy_w,
    cst,
    spread,
    centers,
    out_feat,
    out_rows,
    ext,
    ph,
    fh,
    wgt,
    agg,
    qcols,
    mom,
    rs_buf,
    tb,
    gz_buf,
    field,
    panel,
    send_h,
    recv_h,
    send_r,
    recv_r,
    send_g,
    recv_g,
    send_a,
    recv_a,
):
    zc, xc, slots, entries, channels, n_xy, n_gz = sizes
    atoms = zc * xc * slots
    layers = 2 * zc
    pairs = layers * channels
    share = 2 * channels // n_xy
    f32, bf16 = jnp.float32, jnp.bfloat16
    gz = lax.axis_index("gz")
    xy = lax.axis_index("xy")
    left, right = lax.rem(xy + n_xy - 1, n_xy), lax.rem(xy + 1, n_xy)
    xy_peers = [lax.rem(xy + d, n_xy) for d in range(1, n_xy)]
    gz_peers = [lax.rem(gz + d, n_gz) for d in range(1, n_gz)]
    has_below = gz > 0
    has_above = gz < n_gz - 1

    barrier = pltpu.get_barrier_semaphore()
    for peer in xy_peers:
        pl.semaphore_signal(barrier, inc=1, device_id={"xy": peer}, device_id_type=MESH)
    for peer in gz_peers:
        pl.semaphore_signal(barrier, inc=1, device_id={"gz": peer}, device_id_type=MESH)
    for present, step in ((has_below, -1), (has_above, 1)):

        @pl.when(present)
        def _():
            for side in (left, right):
                pl.semaphore_signal(
                    barrier, inc=1, device_id={"gz": gz + step, "xy": side}, device_id_type=MESH
                )

    cols = jnp.transpose(atom_rows[...])
    kinds = table.shape[0]
    onehot = cols[:, 0:1] == lax.broadcasted_iota(jnp.int32, (atoms, kinds), 1).astype(f32)
    hidden = (feat[...].astype(f32) + dot(onehot.astype(f32).astype(bf16), table[...])).astype(bf16)
    ext[1 : zc + 1, 1 : xc + 1] = hidden.reshape(zc, xc, slots, hidden.shape[1])

    @pl.when(jnp.logical_not(has_below))
    def _():
        ext[0] = jnp.zeros(ext.shape[1:], bf16)

    @pl.when(jnp.logical_not(has_above))
    def _():
        ext[zc + 1] = jnp.zeros(ext.shape[1:], bf16)

    diagonals = 2 * (has_below.astype(jnp.int32) + has_above.astype(jnp.int32))
    pl.semaphore_wait(barrier, n_xy - 1 + n_gz - 1 + diagonals)

    def remote(src, dst, send, recv, target):
        return pltpu.make_async_remote_copy(
            src_ref=src,
            dst_ref=dst,
            send_sem=send,
            recv_sem=recv,
            device_id=target,
            device_id_type=MESH,
        )

    x_copies = [
        remote(ext.at[pl.ds(1, zc), 1], ext.at[pl.ds(1, zc), xc + 1], send_h.at[0], recv_h.at[0], {"xy": left}),
        remote(ext.at[pl.ds(1, zc), xc], ext.at[pl.ds(1, zc), 0], send_h.at[1], recv_h.at[1], {"xy": right}),
    ]

    def z_copies(first, own, ghost, target):
        inner = pl.ds(1, xc)
        return [
            remote(ext.at[own, inner], ext.at[ghost, inner], send_h.at[first], recv_h.at[first], {"gz": target}),
            remote(ext.at[own, 1], ext.at[ghost, xc + 1], send_h.at[first + 1], recv_h.at[first + 1], {"gz": target, "xy": left}),
            remote(ext.at[own, xc], ext.at[ghost, 0], send_h.at[first + 2], recv_h.at[first + 2], {"gz": target, "xy": right}),
        ]

    down = z_copies(2, 1, zc + 1, gz - 1)
    rise = z_copies(5, zc, 0, gz + 1)
    for copy in x_copies:
        copy.start()

    @pl.when(has_below)
    def _():
        for copy in down:
            copy.start()

    @pl.when(has_above)
    def _():
        for copy in rise:
            copy.start()

    wide = 3 * pairs
    charges = dot(hidden, charge_cols[...]).astype(bf16)
    lane = lax.broadcasted_iota(jnp.int32, (atoms, wide), 1)
    row = lax.broadcasted_iota(jnp.int32, (atoms, 1), 0)
    layer = 2 * (row // (xc * slots)) + cols[:, 1:2].astype(jnp.int32)
    qcols[...] = jnp.where(layer == (lane % pairs) // channels, charges.astype(f32), 0.0).astype(bf16)

    cell_x = (xy * xc + (row // slots) % xc).astype(f32)
    coord_x = cell_width * cell_x + cols[:, 3:4]
    coord_y = cols[:, 4:5]
    step = 64
    for start in range(0, atoms, step):
        here = slice(start, start + step)
        at_x, at_y = coord_x[here], coord_y[here]
        sin_0, cos_0 = sincos(at_x * cst[0:1, :KX] + at_y * cst[1:2, :KX])
        ph[here, :KX] = cos_0.astype(bf16)
        ph[here, WAVES : WAVES + KX] = sin_0.astype(bf16)
        sin_x, cos_x = sincos(at_x * cst[3:4, :KX])
        sin_y, cos_y = sincos(at_y * cst[4:5, :KX])
        for b in range(1, len(BLOCKS)):
            cy, sy = cos_y[:, b - 1 : b], sin_y[:, b - 1 : b]
            ph[here, b * KX : (b + 1) * KX] = (cos_x * cy - sin_x * sy).astype(bf16)
            ph[here, WAVES + b * KX : WAVES + (b + 1) * KX] = (sin_x * cy + cos_x * sy).astype(bf16)

    moments = lax.dot_general(
        qcols[:, :pairs], ph[...], (((0,), (0,)), ((), ())), preferred_element_type=f32
    )
    for block in range(n_xy):
        p, c = divmod(block * share, channels)
        for l in range(layers):
            top = l * channels + c
            mom[block, l] = moments[top : top + share, p * WAVES : (p + 1) * WAVES]

    rs_copies = [
        remote(mom.at[peer], rs_buf.at[d], send_r.at[d], recv_r.at[d], {"xy": peer})
        for d, peer in enumerate(xy_peers)
    ]
    for copy in rs_copies:
        copy.start()

    d_all = dist[...]
    count = cols[:, 2:3].astype(jnp.int32)
    entry = lax.broadcasted_iota(jnp.int32, (atoms, entries), 1)
    usable = (entry < count) & (near[...] != 4 * slots + row % slots)
    ratio = d_all * (1.0 / cutoff)
    envelope = 1.0 - ratio * ratio
    wgt[...] = jnp.where(usable, envelope * envelope, 0.0)
    spacing = jnp.dot(d_all, spread[...], precision=lax.Precision.HIGHEST, preferred_element_type=f32)
    gap = spacing - centers[0:1, :]
    basis = jnp.exp(-(gap * gap)).astype(bf16)
    in_rows, in_cols = hidden_in.shape
    for part in range(basis.shape[1] // in_rows):
        for tile in range(in_cols // 256):
            pre = dot(basis[:, part * in_rows : (part + 1) * in_rows], hidden_in[:, tile * 256 : (tile + 1) * 256])
            first = part * in_cols + tile * 256
            fh[:, first : first + 256] = silu(pre).astype(bf16)

    for copy in rs_copies:
        copy.wait()
    total = mom[xy]
    for d in range(n_xy - 1):
        total = total + rs_buf[d]
    mine = [total[l] for l in range(layers)]

    def power(n):
        return cst[5 + n : 6 + n, :]

    tb[0] = sum(mine[l] * power(layers - 1 - l) for l in range(layers))
    tb[1] = sum(mine[l] * power(l) for l in range(layers))
    gz_copies = [
        remote(tb.at[jnp.where(peer > gz, 0, 1)], gz_buf.at[gz], send_g.at[d], recv_g.at[d], {"gz": peer})
        for d, peer in enumerate(gz_peers)
    ]
    for copy in gz_copies:
        copy.start()

    for copy in x_copies:
        copy.wait()

    @pl.when(has_below)
    def _():
        for copy in down:
            copy.wait_send()
        for copy in rise:
            copy.wait_recv()

    @pl.when(has_above)
    def _():
        for copy in rise:
            copy.wait_send()
        for copy in down:
            copy.wait_recv()

    width = feat.shape[1]
    codes = lax.broadcasted_iota(jnp.int32, (slots, 9 * slots), 1)

    def edge_row(z):
        def one(x, carry):
            base = pl.multiple_of((z * xc + x) * slots, slots)
            region = ext[z : z + 3, pl.ds(x, 3)].reshape(9 * slots, width)
            index = near[pl.ds(base, slots), :]
            chosen = jnp.concatenate(
                [
                    jnp.where(index[:, e : e + 1] == codes, 1.0, 0.0).astype(bf16)
                    for e in range(entries)
                ],
                axis=0,
            )
            gathered = dot(chosen, region)
            hid = fh[pl.ds(base, slots), :]
            both = jnp.concatenate(
                [hid[:, p * 128 : (p + 1) * 128] for p in range(hid.shape[1] // 128)], axis=0
            )
            filters = dot(both, hidden_out[...])
            weight = wgt[pl.ds(base, slots), :]
            acc = jnp.zeros((slots, width), f32)
            for e in range(entries):
                part = filters[(e // 2) * slots : (e // 2 + 1) * slots, (e % 2) * width : (e % 2 + 1) * width]
                acc = acc + weight[:, e : e + 1] * part * gathered[e * slots : (e + 1) * slots]
            agg[pl.ds(base, slots), :] = acc.astype(bf16)
            return carry

        lax.fori_loop(0, xc, one, 0)

    for z in range(zc // 2):
        edge_row(z)

    for copy in gz_copies:
        copy.wait()
    span = power(layers)
    blank = jnp.zeros(tb.shape[1:], f32)
    from_below = lax.fori_loop(0, gz, lambda t, s: s * span + gz_buf[t], blank)
    from_above = lax.fori_loop(
        0, n_gz - 1 - gz, lambda t, s: s * span + gz_buf[n_gz - 1 - t], blank
    )
    for l in range(layers):
        value = power(l + 1) * from_below + power(layers - l) * from_above
        for m in range(layers):
            value = value + power(abs(l - m)) * mine[m]
        field[xy, l] = value
    ag_copies = [
        remote(field.at[xy], field.at[xy], send_a.at[d], recv_a.at[d], {"xy": peer})
        for d, peer in enumerate(xy_peers)
    ]
    for copy in ag_copies:
        copy.start()

    for z in range(zc // 2, zc):
        edge_row(z)

    updated = silu(dot(agg[...], update_in[...])).astype(bf16)
    renewed = ext[1 : zc + 1, 1 : xc + 1].reshape(atoms, width).astype(f32) + dot(updated, update_out[...])
    out_feat[...] = renewed.astype(bf16)
    energy = jnp.sum(renewed * energy_w[0:1, :].astype(f32), axis=1, keepdims=True)

    for copy in ag_copies:
        copy.wait()
    wave_x, wave_y, wave_w = cst[0:1, :], cst[1:2, :], cst[2:3, :]
    half = n_xy // 2
    for l in range(layers):
        f_cos = jnp.concatenate([field[b, l] for b in range(half)], axis=0) * wave_w
        f_sin = jnp.concatenate([field[half + b, l] for b in range(half)], axis=0) * wave_w
        lines = ((f_cos, f_sin), (wave_x * f_sin, -wave_x * f_cos), (wave_y * f_sin, -wave_y * f_cos))
        for r, (cos_part, sin_part) in enumerate(lines):
            top = r * pairs + l * channels
            panel[top : top + channels, :WAVES] = cos_part.astype(bf16)
            panel[top : top + channels, WAVES:] = sin_part.astype(bf16)
    evaluated = lax.dot_general(
        ph[...], panel[...], (((1,), (1,)), ((), ())), preferred_element_type=f32
    )
    product = evaluated * qcols[...].astype(f32)
    group = lane // pairs
    sums = [
        jnp.sum(jnp.where(group == r, product, 0.0), axis=1, keepdims=True) for r in range(3)
    ]
    narrow = lax.broadcasted_iota(jnp.int32, (atoms, 128), 1)
    packed = jnp.where(
        narrow == 0, energy + 0.5 * sums[0], jnp.where(narrow == 1, -sums[1], -sums[2])
    )
    out_rows[...] = jnp.transpose(packed)[:8]


def shards(
    n_xy,
    n_gz,
    features,
    species,
    sublayer,
    offsets,
    neighbours,
    neighbour_count,
    distances,
    species_table,
    charge_weight,
    radial_in,
    radial_out,
    update_in,
    update_out,
    energy_weight,
):
    f32, bf16 = jnp.float32, jnp.bfloat16
    zc, xc, slots, width = features.shape
    entries = neighbours.shape[3]
    channels = charge_weight.shape[1]
    atoms = zc * xc * slots
    layers = 2 * zc
    basis_count, radial = radial_in.shape
    share = 2 * channels // n_xy
    cst = wave_constants(cell_width * (xc * n_xy), layers)
    spread = np.kron(np.eye(entries), np.ones((1, basis_count))).astype(np.float32)
    mids = np.float32(cutoff) * np.arange(basis_count).astype(np.float32) / np.float32(basis_count - 1)
    centers = np.tile(mids, (8, entries)).astype(np.float32)
    flat = [species, sublayer, neighbour_count, offsets[0], offsets[1]]
    atom_rows = jnp.stack([a.reshape(atoms).astype(f32) for a in flat] + [jnp.zeros((atoms,), f32)] * 3)
    group = 128 // basis_count
    hidden_in = jnp.kron(jnp.eye(group, dtype=bf16), radial_in)
    hidden_out = jnp.kron(jnp.eye(128 // radial, dtype=bf16), radial_out)
    charge_cols = jnp.tile(charge_weight, (1, 3 * layers))
    sizes = (zc, xc, slots, entries, channels, n_xy, n_gz)
    dma = pltpu.SemaphoreType.DMA
    vmem = pl.BlockSpec(memory_space=pltpu.VMEM)
    out_feat, out_rows = pl.pallas_call(
        functools.partial(kernel, sizes),
        out_shape=(
            jax.ShapeDtypeStruct((atoms, width), bf16),
            jax.ShapeDtypeStruct((8, atoms), f32),
        ),
        in_specs=[vmem] * 14,
        out_specs=(vmem, vmem),
        scratch_shapes=[
            pltpu.VMEM((zc + 2, xc + 2, slots, width), bf16),
            pltpu.VMEM((atoms, 2 * WAVES), bf16),
            pltpu.VMEM((atoms, entries * radial), bf16),
            pltpu.VMEM((atoms, entries), f32),
            pltpu.VMEM((atoms, width), bf16),
            pltpu.VMEM((atoms, 3 * layers * channels), bf16),
            pltpu.VMEM((n_xy, layers, share, WAVES), f32),
            pltpu.VMEM((n_xy - 1, layers, share, WAVES), f32),
            pltpu.VMEM((2, share, WAVES), f32),
            pltpu.VMEM((n_gz, share, WAVES), f32),
            pltpu.VMEM((n_xy, layers, share, WAVES), f32),
            pltpu.VMEM((3 * layers * channels, 2 * WAVES), bf16),
            dma((8,)),
            dma((8,)),
            dma((n_xy - 1,)),
            dma((n_xy - 1,)),
            dma((n_gz - 1,)),
            dma((n_gz - 1,)),
            dma((n_xy - 1,)),
            dma((n_xy - 1,)),
        ],
        compiler_params=pltpu.CompilerParams(
            collective_id=0, has_side_effects=True, vmem_limit_bytes=40 * 1024 * 1024
        ),
        cost_estimate=pl.CostEstimate(flops=2_000_000_000, bytes_accessed=2_000_000, transcendentals=2_000_000),
    )(
        features.reshape(atoms, width),
        atom_rows,
        neighbours.reshape(atoms, entries),
        distances.reshape(atoms, entries),
        species_table,
        charge_cols,
        hidden_in,
        hidden_out,
        update_in,
        update_out,
        energy_weight.reshape(1, width),
        jnp.asarray(cst),
        jnp.asarray(spread),
        jnp.asarray(centers),
    )
    return (
        out_feat.reshape(features.shape),
        out_rows[0].reshape(zc, xc, slots),
        out_rows[1:3].reshape(2, zc, xc, slots),
    )


def solution(mesh):
    atom = P(("groups", "gz"), "xy", None)
    atom_wide = P(("groups", "gz"), "xy", None, None)
    pair = P(None, ("groups", "gz"), "xy", None)
    in_specs = (atom_wide, atom, atom, pair, atom_wide, atom, atom_wide) + (P(),) * 7
    body = functools.partial(shards, mesh.shape["xy"], mesh.shape["gz"])
    return jax.shard_map(
        body, mesh=mesh, in_specs=in_specs, out_specs=(atom_wide, atom, pair), check_vma=False
    )
```

time: 226 us -> 36.8 us (0.16)
  waiting for transfers between devices: 59.1 us -> 0 us
  local copies, waits for them, and re-layouts: 60 us -> 7.21 us
  blocking collectives: 36.2 us -> 0 us
  other arithmetic: 32.5 us -> 0.24 us
  Pallas kernels: 0 us -> 27.9 us
  between operations: 15.2 us -> 0.88 us
  matrix products: 14 us -> 0 us
  starting transfers between devices: 8.37 us -> 0 us
    unnamed x2 -> x0, waiting for transfers between devices: 59.1 us -> none
    gather x2 -> x0, local copies, waits for them, and re-layouts: 53.5 us -> none  [shards(): jnp.take(region, row_index[z_row].reshape(-1), axis=0)]
    all_gather x4 -> x0, blocking collectives: 36.2 us -> none  [the longest x3 18.4 us: carried_in(): gathered = jax.tree.map(lambda a: lax.all_gather(a, axis), part)]
    pallas_call x0 -> x1, Pallas kernels: none -> 27.9 us  [shards(): pl.pallas_call(functools.partial(kernel, sizes), out_shape=(jax.ShapeDtyp...]
    another operation x7 -> x0, other arithmetic: 17.3 us -> none
    dot_general x8 -> x0, matrix products: 14 us -> none  [the longest x2 6.18 us: edge_messages(): jnp.einsum('xsnh,hf->xsnf', filter_hidden, radial_out, preferred_element_...]
    select_n x4 -> x0, other arithmetic: 11.9 us -> none  [the longest x2 11.7 us: shards(): jnp.take(region, row_index[z_row].reshape(-1), axis=0)]
    ppermute x4 -> x0, starting transfers between devices: 8.34 us -> none  [the longest x2 4.95 us: with_halo(): lax.ppermute(tail, axis, [(i, (i + 1) % count) for i in range(ends)])]
  transfers between devices with their start and end apart: 5 -> 0, of which waited for: 1 -> 0; matrix products, arithmetic and copies ran while one was open for 37% -> 0% of each run, Pallas kernels for 0% -> 0%
where the time goes in v1:
time: 36.8 us; the launch traced here: 36.2 us
  Pallas kernels  27.9 us (76%)
  local copies, waits for them, and re-layouts  7.21 us (20%)
  between operations  0.88 us (2%)
    pallas_call x1, Pallas kernels, shards(): pl.pallas_call(functools.partial(kernel, sizes), out_shape=(jax.ShapeDtyp...  27.9 us
    unnamed x34, local copies, waits for them, and re-layouts  4.22 us

profile of v1, /device:TPU:0, one launch (start us, length us, event | category | flops | bytes accessed | tf_op | source)
XLA Modules:
  0.0 36.2 jit_solution(484376886769296864)
XLA Ops:
  0.6 0.7 %fusion.1 = (f32[1,2,8,32]{3,2,1,0:T(8,128)S(1)}, f32[1,2,8,32]{3,2,1,0:T(8,128)S(1)}) fusion(f32[2,2,8,32]{3,2,1,0:T(8,128)} %param.20), kind=kLoop, calls=%fused_computation.7 | loop fusion | bytes 8192 | tf_op jit(solution)/shard_map/slice | solution.py:423
  1.3 0.1 stack_reshape_squeeze.6
  1.4 0.1 stack_reshape_squeeze.7
  1.5 0.6 %copy-done.11 = s32[2,8,32]{2,1,0:T(8,128)S(1)} copy-done((s32[2,8,32]{2,1,0:T(8,128)S(1)}, s32[2,8,32]{2,1,0:T(8,128)}, u32[]{:S(2)}) %copy-start.11) | copy-done | bytes 2072
  2.1 0.1 convert_element_type.54
  2.2 0.6 %copy-done.12 = s32[2,8,32]{2,1,0:T(8,128)S(1)} copy-done((s32[2,8,32]{2,1,0:T(8,128)S(1)}, s32[2,8,32]{2,1,0:T(8,128)}, u32[]{:S(2)}) %copy-start.12) | copy-done | bytes 2072
  2.8 0.1 convert_element_type.56
  2.9 0.6 %copy-done.13 = s32[2,8,32]{2,1,0:T(8,128)S(1)} copy-done((s32[2,8,32]{2,1,0:T(8,128)S(1)}, s32[2,8,32]{2,1,0:T(8,128)}, u32[]{:S(2)}) %copy-start.13) | copy-done | bytes 2072
  3.5 0.1 convert_element_type.58
  3.7 0.7 %copy-done.15 = bf16[8,64]{1,0:T(8,128)(2,1)S(1)} copy-done((bf16[8,64]{1,0:T(8,128)(2,1)S(1)}, bf16[8,64]{1,0:T(8,128)(2,1)}, u32[]{:S(2)}) %copy-start.15) | copy-done | bytes 1048
  4.3 0.1 broadcast_multiply_fusion
  4.5 0.0 copy-start.7
  4.5 0.0 copy-start.8
  4.5 0.0 copy-start.9
  4.5 0.3 mul.51.hidden_in
  4.9 0.3 copy-done.10
  5.2 0.1 broadcast_multiply_fusion.1
  5.3 0.1 copy.21.charge_cols
  5.5 0.3 copy-done
  5.9 0.4 %copy-done.2 = bf16[2,8,32,128]{3,2,1,0:T(8,128)(2,1)S(1)} copy-done((bf16[2,8,32,128]{3,2,1,0:T(8,128)(2,1)S(1)}, bf16[2,8,32,128]{3,2,1,0:T(8,128)(2,1)}, u32[]{:S(2)}) %copy-start.2) | copy-done | bytes 131096
  6.3 27.9 %shard_map.184 = (bf16[512,128]{1,0:T(8,128)(2,1)S(1)}, f32[8,512]{1,0:T(8,128)S(1)}) custom-call(bf16[512,128]{1,0:T(8,128)(2,1)S(1)} %bitcast.21, f32[8,512]{1,0:T(8,128)S(1)} %stack.10.atom_rows, s32[512,32]{1,0:T(8,128)S(1)} %bitcast.19, f32[512,32]{1,0:T(8,128)S(1)} %bitcast.20, bf16[8,128]{1,0:T(8,128)(2,1)S(1)} %copy-done.5, ...), custom_call_target="tpu_custom_call" | custom-call | flops 2000000000 | bytes 2000000 | tf_op jit(solution)/shard_map/pallas_call | solution.py:432
  34.2 0.7 %reshape.97 = f32[2,2,8,32]{3,2,1,0:T(8,128)} reshape(f32[2,512]{1,0:T(2,128)S(1)} %slice.15) | data formatting | bytes 8192 | tf_op jit(solution)/shard_map/reshape | solution.py:485
  34.9 0.7 %reshape_squeeze.3 = f32[2,8,32]{2,1,0:T(8,128)} reshape(f32[512]{0:T(512)S(1)} %slice_reduce_fusion) | data formatting | bytes 4096 | tf_op jit(solution)/shard_map/reshape;squeeze | solution.py:484
  35.6 0.7 %copy.26 = bf16[2,8,32,128]{3,2,1,0:T(8,128)(2,1)} copy(bf16[2,8,32,128]{3,2,1,0:T(8,128)(2,1)S(1)} %bitcast.17) | data formatting | bytes 262144
  (34 shorter events, 0.2 us)
Async XLA Ops:
  1.4 0.7 %copy-start.11 = (s32[2,8,32]{2,1,0:T(8,128)S(1)}, s32[2,8,32]{2,1,0:T(8,128)}, u32[]{:S(2)}) copy-start(s32[2,8,32]{2,1,0:T(8,128)} %param.18) | copy-start | bytes 6148
  2.1 0.7 %copy-start.12 = (s32[2,8,32]{2,1,0:T(8,128)S(1)}, s32[2,8,32]{2,1,0:T(8,128)}, u32[]{:S(2)}) copy-start(s32[2,8,32]{2,1,0:T(8,128)} %param.19) | copy-start | bytes 6148
  2.8 0.7 %copy-start.13 = (s32[2,8,32]{2,1,0:T(8,128)S(1)}, s32[2,8,32]{2,1,0:T(8,128)}, u32[]{:S(2)}) copy-start(s32[2,8,32]{2,1,0:T(8,128)} %param.22) | copy-start | bytes 6148
  3.7 0.7 %copy-start.15 = (bf16[8,64]{1,0:T(8,128)(2,1)S(1)}, bf16[8,64]{1,0:T(8,128)(2,1)}, u32[]{:S(2)}) copy-start(bf16[8,64]{1,0:T(8,128)(2,1)} %param.26) | copy-start | bytes 3076
  4.4 0.7 %copy-start.10 = (bf16[64,128]{1,0:T(8,128)(2,1)S(1)}, bf16[64,128]{1,0:T(8,128)(2,1)}, u32[]{:S(2)}) copy-start(bf16[64,128]{1,0:T(8,128)(2,1)} %param.27) | copy-start | bytes 49156
  4.5 0.9 %copy-start.14 = (bf16[128,16]{0,1:T(8,128)(2,1)S(1)}, bf16[128,16]{0,1:T(8,128)(2,1)}, u32[]{:S(2)}) copy-start(bf16[128,16]{0,1:T(8,128)(2,1)} %param.25) | copy-start | bytes 12292
  4.5 1.0 %copy-start.1 = (f32[2,8,32,32]{3,2,1,0:T(8,128)S(1)}, f32[2,8,32,32]{3,2,1,0:T(8,128)}, u32[]{:S(2)}) copy-start(f32[2,8,32,32]{3,2,1,0:T(8,128)} %param.23) | copy-start | bytes 196612
  4.5 1.0 %copy-start.3 = (bf16[128,256]{1,0:T(8,128)(2,1)S(1)}, bf16[128,256]{1,0:T(8,128)(2,1)}, u32[]{:S(2)}) copy-start(bf16[128,256]{1,0:T(8,128)(2,1)} %update_in.1) | copy-start | bytes 196612
  4.5 1.0 %copy-start.4 = (bf16[256,128]{1,0:T(8,128)(2,1)S(1)}, bf16[256,128]{1,0:T(8,128)(2,1)}, u32[]{:S(2)}) copy-start(bf16[256,128]{1,0:T(8,128)(2,1)} %update_out.1) | copy-start | bytes 196612
  4.5 1.0 %copy-start.7 = (f32[16,640]{1,0:T(8,128)S(1)}, f32[16,640]{1,0:T(8,128)}, u32[]{:S(2)}) copy-start(f32[16,640]{1,0:T(8,128)} %constant.3.clone.cst) | copy-start | bytes 122884
  4.5 1.0 %copy-start.8 = (f32[32,256]{1,0:T(8,128)S(1)}, f32[32,256]{1,0:T(8,128)}, u32[]{:S(2)}) copy-start(f32[32,256]{1,0:T(8,128)} %constant.10.clone.spread) | copy-start | bytes 98308
  4.5 1.0 %copy-start.9 = (f32[8,256]{1,0:T(8,128)S(1)}, f32[8,256]{1,0:T(8,128)}, u32[]{:S(2)}) copy-start(f32[8,256]{1,0:T(8,128)} %constant.11.clone.centers) | copy-start | bytes 24580
  4.9 1.0 %copy-start = (s32[2,8,32,32]{3,2,1,0:T(8,128)S(1)}, s32[2,8,32,32]{3,2,1,0:T(8,128)}, u32[]{:S(2)}) copy-start(s32[2,8,32,32]{3,2,1,0:T(8,128)} %param.21) | copy-start | bytes 196612
  5.3 1.0 %copy-start.2 = (bf16[2,8,32,128]{3,2,1,0:T(8,128)(2,1)S(1)}, bf16[2,8,32,128]{3,2,1,0:T(8,128)(2,1)}, u32[]{:S(2)}) copy-start(bf16[2,8,32,128]{3,2,1,0:T(8,128)(2,1)} %param.17) | copy-start | bytes 393220
  5.5 0.8 %copy-start.5 = (bf16[8,128]{1,0:T(8,128)(2,1)S(1)}, bf16[8,128]{1,0:T(8,128)(2,1)}, u32[]{:S(2)}) copy-start(bf16[8,128]{1,0:T(8,128)(2,1)} %table.1) | copy-start | bytes 6148
  5.5 0.8 %copy-start.6 = (bf16[128]{0:T(256)(128)(2,1)S(1)}, bf16[128]{0:T(256)(128)(2,1)}, u32[]{:S(2)}) copy-start(bf16[128]{0:T(256)(128)(2,1)} %param.30) | copy-start | bytes 772

commit v2 on v1

v2 whole, which is shorter than its diff:
```python
import functools
import math

import jax
import jax.numpy as jnp
import numpy as np
from jax import lax
from jax.experimental import pallas as pl
from jax.experimental.pallas import tpu as pltpu
from jax.sharding import PartitionSpec as P

KX = 128
KY = 8
MESH = pl.DeviceIdType.MESH

cell_width = 11.0
layer_depth = 5.5
screening = 0.025
smearing = 1.0
coupling = 0.25
cutoff = 8.0

BLOCKS = (4, 0, 5, 6, 7)
LANES = 384


def wave_constants(width_x, layers, n_xy):
    f32 = np.float32
    per = KX // n_xy

    def factors(index_x, index_y, count):
        wave_x = f32(2.0 * math.pi / width_x) * (index_x - KX // 2).astype(f32)
        wave_y = f32(2.0 * math.pi / cell_width) * (index_y - KY // 2).astype(f32)
        square = wave_x * wave_x + wave_y * wave_y
        screened = np.sqrt(square + f32(screening * screening))
        weight = f32(coupling * (2.0 * math.pi / (width_x * cell_width))) * np.exp(
            f32(-0.5 * smearing * smearing) * square
        )
        return wave_x, wave_y, weight / screened * count, screened

    strips = []
    for strip in range(n_xy):
        own = np.arange(strip * per, (strip + 1) * per)
        index_x = np.tile(own, len(BLOCKS) - 1)
        index_y = np.repeat(np.array(BLOCKS[1:]), per)
        count = np.where((index_y > KY // 2) & (index_x > 0), 2.0, 1.0).astype(f32)
        part_a = factors(index_x, index_y, count)
        index_x, index_y = own.copy(), np.full(per, KY // 2)
        count = np.where((own > 0) & (own < KX // 2), 2.0, 1.0).astype(f32)
        count[own > KX // 2] = 0.0
        for spare, j in enumerate((1, 2, 3)):
            place = KX // 2 + 1 + spare
            count[own == place] = 1.0
            index_y[own == place] = j
            index_x[own == place] = 0
        part_b = factors(index_x, index_y, count)
        lanes = []
        for one, two in zip(part_a, part_b):
            one = np.pad(one, (0, 128 - one.size))
            two = np.pad(two, (0, 64 - two.size))
            lanes.append(np.concatenate([one, one, two, two]))
        wave_x, wave_y, weight, screened = lanes
        sign = np.repeat(np.array([1, -1, 1, -1], f32), [128, 128, 64, 64])
        powers = [np.exp(-screened * f32(layer_depth) * f32(n)) for n in range(layers + 1)]
        rows = [wave_x, wave_y, weight, sign * wave_x, sign * wave_y] + powers
        rows += [np.zeros(LANES, f32)] * (-len(rows) % 8)
        strips.append(np.stack(rows))
    return np.stack(strips).astype(f32)


def reduced(angle):
    turns = jnp.floor(angle * (2.0 / math.pi) + 0.5)
    rest = angle - turns * 1.5703125
    rest = rest - turns * 4.8375129699707031e-4
    rest = rest - turns * 7.5497899548918822e-8
    square = rest * rest
    sine = rest + rest * square * (
        (-1.9515295891e-4 * square + 8.3321608736e-3) * square - 1.6666654611e-1
    )
    cosine = (1.0 - 0.5 * square) + square * square * (
        (2.443315711809948e-5 * square - 1.388731625493765e-3) * square + 4.166664568298827e-2
    )
    return turns.astype(jnp.int32), sine, cosine


def at_quadrant(quadrant, sine, cosine):
    value = jnp.where((quadrant & 1) == 1, cosine, sine)
    return jnp.where((quadrant & 2) == 2, -value, value)


def silu(value):
    half = 0.5 * value
    return half + half * jnp.tanh(half)


def dot(a, b):
    return jnp.dot(a, b, preferred_element_type=jnp.float32)


def kernel(
    sizes,
    feat,
    species,
    sublayer,
    counts,
    offsets,
    near,
    dist,
    table,
    charge_w,
    radial_in,
    radial_out,
    update_in,
    update_out,
    energy_w,
    cst,
    centers,
    out_feat,
    out_energy,
    out_forces,
    ext,
    ph,
    fh,
    wgt,
    agg,
    own_rows,
    coords,
    q_all,
    qw,
    tb,
    gz_buf,
    mine,
    panel,
    part,
    part_buf,
    send_h,
    recv_h,
    send_c,
    recv_c,
    send_q,
    recv_q,
    send_g,
    recv_g,
    send_p,
    recv_p,
):
    zc, xc, slots, entries, channels, n_xy, n_gz = sizes
    cells = zc * xc
    atoms = cells * slots
    layers = 2 * zc
    pairs = layers * channels
    f32, bf16, i32 = jnp.float32, jnp.bfloat16, jnp.int32
    exact = lax.Precision.HIGHEST
    iota = lax.broadcasted_iota
    width = feat.shape[1]
    gz = lax.axis_index("gz")
    xy = lax.axis_index("xy")
    left, right = lax.rem(xy + n_xy - 1, n_xy), lax.rem(xy + 1, n_xy)
    xy_peers = [lax.rem(xy + d, n_xy) for d in range(1, n_xy)]
    gz_peers = [lax.rem(gz + d, n_gz) for d in range(1, n_gz)]
    has_below = gz > 0
    has_above = gz < n_gz - 1

    barrier = pltpu.get_barrier_semaphore()
    for peer in xy_peers:
        pl.semaphore_signal(barrier, inc=1, device_id={"xy": peer}, device_id_type=MESH)
    for peer in gz_peers:
        pl.semaphore_signal(barrier, inc=1, device_id={"gz": peer}, device_id_type=MESH)
    for present, step in ((has_below, -1), (has_above, 1)):

        @pl.when(present)
        def _():
            for side in (left, right):
                pl.semaphore_signal(
                    barrier, inc=1, device_id={"gz": gz + step, "xy": side}, device_id_type=MESH
                )

    unfold = (iota(i32, (slots, atoms), 1) % slots == iota(i32, (slots, atoms), 0)).astype(f32)
    own_cell = iota(i32, (cells, atoms), 1) // slots == iota(i32, (cells, atoms), 0)
    stacked = jnp.concatenate(
        [species[...].astype(f32), sublayer[...].astype(f32), counts[...].astype(f32), offsets[...]],
        axis=0,
    )
    wide = jnp.dot(stacked, unfold, precision=exact, preferred_element_type=f32)
    kind_row, sub_row, count_row, x_row, y_row = [
        jnp.sum(jnp.where(own_cell, wide[i * cells : (i + 1) * cells], 0.0), axis=0, keepdims=True)
        for i in range(5)
    ]
    atom_cell = iota(i32, (1, atoms), 1) // slots
    x_row = cell_width * (xy * xc + atom_cell % xc).astype(f32) + x_row
    layer_row = sub_row + (2 * (atom_cell // xc)).astype(f32)
    blank = jnp.zeros((3, atoms), f32)
    rows = jnp.concatenate([x_row, y_row, layer_row, kind_row, count_row, blank], axis=0)
    coords[xy] = rows
    cols = jnp.transpose(rows)

    kinds = table.shape[0]
    onehot = cols[:, 3:4] == iota(i32, (atoms, kinds), 1).astype(f32)
    hidden = (feat[...].astype(f32) + dot(onehot.astype(f32).astype(bf16), table[...])).astype(bf16)
    ext[1 : zc + 1, 1 : xc + 1] = hidden.reshape(zc, xc, slots, width)
    q_all[xy] = lax.dot_general(
        charge_w[...], hidden, (((1,), (1,)), ((), ())), preferred_element_type=f32
    ).astype(bf16)

    @pl.when(jnp.logical_not(has_below))
    def _():
        ext[0] = jnp.zeros(ext.shape[1:], bf16)

    @pl.when(jnp.logical_not(has_above))
    def _():
        ext[zc + 1] = jnp.zeros(ext.shape[1:], bf16)

    diagonals = 2 * (has_below.astype(i32) + has_above.astype(i32))
    pl.semaphore_wait(barrier, n_xy - 1 + n_gz - 1 + diagonals)

    def remote(src, dst, send, recv, target):
        return pltpu.make_async_remote_copy(
            src_ref=src,
            dst_ref=dst,
            send_sem=send,
            recv_sem=recv,
            device_id=target,
            device_id_type=MESH,
        )

    strip_copies = []
    for d, peer in enumerate(xy_peers):
        strip_copies += [
            remote(coords.at[xy], coords.at[xy], send_c.at[d], recv_c.at[d], {"xy": peer}),
            remote(q_all.at[xy], q_all.at[xy], send_q.at[d], recv_q.at[d], {"xy": peer}),
        ]
    for copy in strip_copies:
        copy.start()

    inner = pl.ds(1, zc)
    x_copies = [
        remote(ext.at[inner, 1], ext.at[inner, xc + 1], send_h.at[0], recv_h.at[0], {"xy": left}),
        remote(ext.at[inner, xc], ext.at[inner, 0], send_h.at[1], recv_h.at[1], {"xy": right}),
    ]

    def z_copies(first, own, ghost, target):
        strip = pl.ds(1, xc)
        return [
            remote(ext.at[own, strip], ext.at[ghost, strip], send_h.at[first], recv_h.at[first], {"gz": target}),
            remote(ext.at[own, 1], ext.at[ghost, xc + 1], send_h.at[first + 1], recv_h.at[first + 1], {"gz": target, "xy": left}),
            remote(ext.at[own, xc], ext.at[ghost, 0], send_h.at[first + 2], recv_h.at[first + 2], {"gz": target, "xy": right}),
        ]

    down = z_copies(2, 1, zc + 1, gz - 1)
    rise = z_copies(5, zc, 0, gz + 1)
    for copy in x_copies:
        copy.start()

    @pl.when(has_below)
    def _():
        for copy in down:
            copy.start()

    @pl.when(has_above)
    def _():
        for copy in rise:
            copy.start()

    def strip_phases(strip):
        at = jnp.transpose(coords[strip])
        turn = jnp.where(iota(i32, (1, 128), 1) < 64, 1, 0)
        step = 64
        for start in range(0, atoms, step):
            here = slice(start, start + step)
            at_x, at_y = at[here, 0:1], at[here, 1:2]
            lines = pl.ds(strip * atoms + start, step)
            quadrant, sine, cosine = reduced(at_x * cst[xy, 0:1, :128] + at_y * cst[xy, 1:2, :128])
            ph[lines, :128] = at_quadrant(quadrant + 1, sine, cosine).astype(bf16)
            ph[lines, 128:256] = at_quadrant(quadrant, sine, cosine).astype(bf16)
            quadrant, sine, cosine = reduced(at_x * cst[xy, 0:1, 256:] + at_y * cst[xy, 1:2, 256:])
            ph[lines, 256:] = at_quadrant(quadrant + turn, sine, cosine).astype(bf16)

    def strip_moments(strip):
        layer = coords[strip][2:3]
        charges = q_all[strip].astype(f32)
        weighted = jnp.concatenate(
            [jnp.where(layer == float(l), charges, 0.0) for l in range(layers)], axis=0
        ).astype(bf16)
        qw[strip] = weighted
        return dot(weighted, ph[pl.ds(strip * atoms, atoms), :])

    strip_phases(xy)
    total = strip_moments(xy)

    d_all = dist[...]
    slot = iota(i32, (atoms, 1), 0) % slots
    entry = iota(i32, (atoms, entries), 1)
    usable = (entry < cols[:, 4:5].astype(i32)) & (near[...] != 4 * slots + slot)
    ratio = d_all * (1.0 / cutoff)
    envelope = 1.0 - ratio * ratio
    wgt[...] = jnp.where(usable, envelope * envelope, 0.0)
    basis_count, radial = radial_in.shape
    spread_shape = (entries, entries * basis_count)
    spread = (iota(i32, spread_shape, 1) // basis_count == iota(i32, spread_shape, 0)).astype(f32)
    spacing = jnp.dot(d_all, spread, precision=exact, preferred_element_type=f32)
    gap = spacing - centers[0:1, :]
    basis = jnp.exp(-(gap * gap)).astype(bf16)
    group = 128 // basis_count
    tall = jnp.concatenate([radial_in[...].astype(f32)] * group, axis=0)
    flat = jnp.concatenate([tall] * group, axis=1)
    diagonal = iota(i32, flat.shape, 0) // basis_count == iota(i32, flat.shape, 1) // radial
    hidden_in = jnp.where(diagonal, flat, 0.0).astype(bf16)
    for block in range(entries // group):
        for tile in range(flat.shape[1] // 256):
            pre = dot(basis[:, block * 128 : (block + 1) * 128], hidden_in[:, tile * 256 : (tile + 1) * 256])
            first = block * flat.shape[1] + tile * 256
            fh[:, first : first + 256] = silu(pre).astype(bf16)
    pack = 128 // radial
    tall = jnp.concatenate([radial_out[...].astype(f32)] * pack, axis=0)
    flat = jnp.concatenate([tall] * pack, axis=1)
    diagonal = iota(i32, flat.shape, 0) // radial == iota(i32, flat.shape, 1) // width
    hidden_out = jnp.where(diagonal, flat, 0.0).astype(bf16)

    for copy in strip_copies:
        copy.wait()

    def add_strip(d, total):
        strip = lax.rem(xy + d, n_xy)
        strip_phases(strip)
        return total + strip_moments(strip)

    total = lax.fori_loop(1, n_xy, add_strip, total)
    mine[...] = total

    def power(n):
        return cst[xy, 5 + n : 6 + n, :]

    def layer_moments(l):
        return mine[l * channels : (l + 1) * channels, :]

    tb[0] = sum(layer_moments(l) * power(layers - 1 - l) for l in range(layers))
    tb[1] = sum(layer_moments(l) * power(l) for l in range(layers))
    gz_copies = [
        remote(tb.at[jnp.where(peer > gz, 0, 1)], gz_buf.at[gz], send_g.at[d], recv_g.at[d], {"gz": peer})
        for d, peer in enumerate(gz_peers)
    ]
    for copy in gz_copies:
        copy.start()

    for copy in x_copies:
        copy.wait()

    @pl.when(has_below)
    def _():
        for copy in down:
            copy.wait_send()
        for copy in rise:
            copy.wait_recv()

    @pl.when(has_above)
    def _():
        for copy in rise:
            copy.wait_send()
        for copy in down:
            copy.wait_recv()

    codes = iota(i32, (slots, 9 * slots), 1)

    def edge_row(z):
        def one(x, carry):
            base = pl.multiple_of((z * xc + x) * slots, slots)
            region = ext[z : z + 3, pl.ds(x, 3)].reshape(9 * slots, width)
            index = near[pl.ds(base, slots), :]
            chosen = jnp.concatenate(
                [
                    jnp.where(index[:, e : e + 1] == codes, 1.0, 0.0).astype(bf16)
                    for e in range(entries)
                ],
                axis=0,
            )
            gathered = dot(chosen, region)
            hid = fh[pl.ds(base, slots), :]
            both = jnp.concatenate(
                [hid[:, p * 128 : (p + 1) * 128] for p in range(hid.shape[1] // 128)], axis=0
            )
            filters = dot(both, hidden_out)
            weight = wgt[pl.ds(base, slots), :]
            acc = jnp.zeros((slots, width), f32)
            for e in range(entries):
                row, col = (e // pack) * slots, (e % pack) * width
                filtered = weight[:, e : e + 1] * filters[row : row + slots, col : col + width]
                acc = acc + filtered * gathered[e * slots : (e + 1) * slots]
            agg[pl.ds(base, slots), :] = acc.astype(bf16)
            return carry

        lax.fori_loop(0, xc, one, 0)

    for z in range(zc // 2):
        edge_row(z)

    for copy in gz_copies:
        copy.wait()
    span = power(layers)
    none = jnp.zeros(tb.shape[1:], f32)
    from_below = lax.fori_loop(0, gz, lambda t, s: s * span + gz_buf[t], none)
    from_above = lax.fori_loop(0, n_gz - 1 - gz, lambda t, s: s * span + gz_buf[n_gz - 1 - t], none)
    for l in range(layers):
        value = power(l + 1) * from_below + power(layers - l) * from_above
        for m in range(layers):
            value = value + power(abs(l - m)) * layer_moments(m)
        value = value * cst[xy, 2:3, :]
        swapped = jnp.concatenate(
            [value[:, 128:256], value[:, :128], value[:, 320:], value[:, 256:320]], axis=1
        )
        lines = (value, cst[xy, 3:4, :] * swapped, cst[xy, 4:5, :] * swapped)
        for r, line in enumerate(lines):
            top = r * pairs + l * channels
            panel[top : top + channels, :] = line.astype(bf16)

    def strip_sums(strip):
        evaluated = lax.dot_general(
            panel[...],
            ph[pl.ds(strip * atoms, atoms), :],
            (((1,), (1,)), ((), ())),
            preferred_element_type=f32,
        )
        charges = qw[strip].astype(f32)
        lines = [
            jnp.sum(evaluated[r * pairs : (r + 1) * pairs] * charges, axis=0, keepdims=True)
            for r in range(3)
        ]
        return jnp.concatenate(lines + [jnp.zeros((5, atoms), f32)], axis=0)

    part_copies = []
    for d, peer in enumerate(xy_peers):
        part[d] = strip_sums(peer)
        copy = remote(part.at[d], part_buf.at[d], send_p.at[d], recv_p.at[d], {"xy": peer})
        copy.start()
        part_copies.append(copy)
    own_rows[...] = strip_sums(xy)

    for z in range(zc // 2, zc):
        edge_row(z)

    updated = silu(dot(agg[...], update_in[...])).astype(bf16)
    renewed = ext[1 : zc + 1, 1 : xc + 1].reshape(atoms, width).astype(f32) + dot(updated, update_out[...])
    out_feat[...] = renewed.astype(bf16)
    readout = jnp.broadcast_to(energy_w[0:1, :].astype(f32), (8, width))
    energy = lax.dot_general(
        readout, renewed, (((1,), (1,)), ((), ())), precision=exact, preferred_element_type=f32
    )

    for copy in part_copies:
        copy.wait()
    sums = own_rows[...]
    for d in range(n_xy - 1):
        sums = sums + part_buf[d]
    finals = (energy[0:1] + 0.5 * sums[0:1], -sums[1:2], -sums[2:3])
    spread_out = jnp.concatenate([jnp.where(own_cell, line, 0.0) for line in finals], axis=0)
    folded = lax.dot_general(
        spread_out, unfold, (((1,), (1,)), ((), ())), precision=exact, preferred_element_type=f32
    )
    out_energy[...] = folded[:cells]
    out_forces[...] = folded[cells:]


def shards(
    n_xy,
    n_gz,
    features,
    species,
    sublayer,
    offsets,
    neighbours,
    neighbour_count,
    distances,
    species_table,
    charge_weight,
    radial_in,
    radial_out,
    update_in,
    update_out,
    energy_weight,
):
    f32, bf16 = jnp.float32, jnp.bfloat16
    zc, xc, slots, width = features.shape
    entries = neighbours.shape[3]
    channels = charge_weight.shape[1]
    cells = zc * xc
    atoms = cells * slots
    layers = 2 * zc
    pairs = layers * channels
    basis_count, radial = radial_in.shape
    cst = wave_constants(cell_width * (xc * n_xy), layers, n_xy)
    mids = np.float32(cutoff) * np.arange(basis_count).astype(np.float32) / np.float32(basis_count - 1)
    centers = np.tile(mids, (8, entries)).astype(np.float32)
    sizes = (zc, xc, slots, entries, channels, n_xy, n_gz)
    dma = pltpu.SemaphoreType.DMA
    vmem = pl.BlockSpec(memory_space=pltpu.VMEM)
    out_feat, energy, forces = pl.pallas_call(
        functools.partial(kernel, sizes),
        out_shape=(
            jax.ShapeDtypeStruct((atoms, width), bf16),
            jax.ShapeDtypeStruct((cells, slots), f32),
            jax.ShapeDtypeStruct((2 * cells, slots), f32),
        ),
        in_specs=[vmem] * 16,
        out_specs=(vmem, vmem, vmem),
        scratch_shapes=[
            pltpu.VMEM((zc + 2, xc + 2, slots, width), bf16),
            pltpu.VMEM((n_xy * atoms, LANES), bf16),
            pltpu.VMEM((atoms, entries * radial), bf16),
            pltpu.VMEM((atoms, entries), f32),
            pltpu.VMEM((atoms, width), bf16),
            pltpu.VMEM((8, atoms), f32),
            pltpu.VMEM((n_xy, 8, atoms), f32),
            pltpu.VMEM((n_xy, channels, atoms), bf16),
            pltpu.VMEM((n_xy, pairs, atoms), bf16),
            pltpu.VMEM((2, channels, LANES), f32),
            pltpu.VMEM((n_gz, channels, LANES), f32),
            pltpu.VMEM((pairs, LANES), f32),
            pltpu.VMEM((3 * pairs, LANES), bf16),
            pltpu.VMEM((n_xy - 1, 8, atoms), f32),
            pltpu.VMEM((n_xy - 1, 8, atoms), f32),
            dma((8,)),
            dma((8,)),
            dma((n_xy - 1,)),
            dma((n_xy - 1,)),
            dma((n_xy - 1,)),
            dma((n_xy - 1,)),
            dma((n_gz - 1,)),
            dma((n_gz - 1,)),
            dma((n_xy - 1,)),
            dma((n_xy - 1,)),
        ],
        compiler_params=pltpu.CompilerParams(
            collective_id=0, has_side_effects=True, vmem_limit_bytes=40 * 1024 * 1024
        ),
        cost_estimate=pl.CostEstimate(flops=2_000_000_000, bytes_accessed=2_000_000, transcendentals=2_000_000),
    )(
        features.reshape(atoms, width),
        species.reshape(cells, slots),
        sublayer.reshape(cells, slots),
        neighbour_count.reshape(cells, slots),
        offsets.reshape(2 * cells, slots),
        neighbours.reshape(atoms, entries),
        distances.reshape(atoms, entries),
        species_table,
        charge_weight.T,
        radial_in,
        radial_out,
        update_in,
        update_out,
        energy_weight.reshape(1, width),
        jnp.asarray(cst),
        jnp.asarray(centers),
    )
    return (
        out_feat.reshape(features.shape),
        energy.reshape(species.shape),
        forces.reshape((2,) + species.shape),
    )


def solution(mesh):
    atom = P(("groups", "gz"), "xy", None)
    atom_wide = P(("groups", "gz"), "xy", None, None)
    pair = P(None, ("groups", "gz"), "xy", None)
    in_specs = (atom_wide, atom, atom, pair, atom_wide, atom, atom_wide) + (P(),) * 7
    body = functools.partial(shards, mesh.shape["xy"], mesh.shape["gz"])
    return jax.shard_map(
        body, mesh=mesh, in_specs=in_specs, out_specs=(atom_wide, atom, pair), check_vma=False
    )
```

time: 36.8 us -> 38.2 us (1.038)
  the two profiles are of different devices: /device:TPU:0 before, /device:TPU:1 now
where the time goes in v2:
time: 38.2 us; the launch traced here: 37.6 us
  Pallas kernels  23.4 us (61%)
  local copies, waits for them, and re-layouts  13.5 us (35%)
  between operations  0.68 us (2%)
    pallas_call x1, Pallas kernels, shards(): pl.pallas_call(functools.partial(kernel, sizes), out_shape=(jax.ShapeDtyp...  23.4 us
    unnamed x35, local copies, waits for them, and re-layouts  13.5 us

profile of v2, /device:TPU:1, one launch (start us, length us, event | category | flops | bytes accessed | tf_op | source)
XLA Modules:
  0.0 37.6 jit_solution(3350072834851080416)
XLA Ops:
  0.6 0.0 copy-start.5
  0.6 0.0 copy-start.13
  0.7 0.7 %copy-done.5 = f32[2,2,8,32]{3,2,1,0:T(8,128)S(1)} copy-done((f32[2,2,8,32]{3,2,1,0:T(8,128)S(1)}, f32[2,2,8,32]{3,2,1,0:T(8,128)}, u32[]{:S(2)}) %copy-start.5) | copy-done | bytes 4120
  1.4 0.0 copy-done.13
  1.4 0.0 copy-start
  1.4 0.9 %copy-done = s32[2,8,32,32]{3,2,1,0:T(8,128)S(1)} copy-done((s32[2,8,32,32]{3,2,1,0:T(8,128)S(1)}, s32[2,8,32,32]{3,2,1,0:T(8,128)}, u32[]{:S(2)}) %copy-start) | copy-done | bytes 65560
  2.3 0.0 copy-start.1
  2.3 0.9 %copy-done.1 = f32[2,8,32,32]{3,2,1,0:T(8,128)S(1)} copy-done((f32[2,8,32,32]{3,2,1,0:T(8,128)S(1)}, f32[2,8,32,32]{3,2,1,0:T(8,128)}, u32[]{:S(2)}) %copy-start.1) | copy-done | bytes 65560
  3.3 0.9 %copy-done.2 = bf16[2,8,32,128]{3,2,1,0:T(8,128)(2,1)S(1)} copy-done((bf16[2,8,32,128]{3,2,1,0:T(8,128)(2,1)S(1)}, bf16[2,8,32,128]{3,2,1,0:T(8,128)(2,1)}, u32[]{:S(2)}) %copy-start.2) | copy-done | bytes 131096
  4.2 0.8 %copy-done.3 = bf16[128,256]{1,0:T(8,128)(2,1)S(1)} copy-done((bf16[128,256]{1,0:T(8,128)(2,1)S(1)}, bf16[128,256]{1,0:T(8,128)(2,1)}, u32[]{:S(2)}) %copy-start.3) | copy-done | bytes 65560
  5.0 0.8 %copy-done.4 = bf16[256,128]{1,0:T(8,128)(2,1)S(1)} copy-done((bf16[256,128]{1,0:T(8,128)(2,1)S(1)}, bf16[256,128]{1,0:T(8,128)(2,1)}, u32[]{:S(2)}) %copy-start.4) | copy-done | bytes 65560
  5.8 0.7 %copy-done.6 = bf16[64,128]{1,0:T(8,128)(2,1)S(1)} copy-done((bf16[64,128]{1,0:T(8,128)(2,1)S(1)}, bf16[64,128]{1,0:T(8,128)(2,1)}, u32[]{:S(2)}) %copy-start.6) | copy-done | bytes 16408
  6.6 0.7 %copy-done.7 = s32[2,8,32]{2,1,0:T(8,128)S(1)} copy-done((s32[2,8,32]{2,1,0:T(8,128)S(1)}, s32[2,8,32]{2,1,0:T(8,128)}, u32[]{:S(2)}) %copy-start.7) | copy-done | bytes 2072
  7.3 0.7 %copy-done.8 = s32[2,8,32]{2,1,0:T(8,128)S(1)} copy-done((s32[2,8,32]{2,1,0:T(8,128)S(1)}, s32[2,8,32]{2,1,0:T(8,128)}, u32[]{:S(2)}) %copy-start.8) | copy-done | bytes 2072
  8.0 0.7 %copy-done.9 = s32[2,8,32]{2,1,0:T(8,128)S(1)} copy-done((s32[2,8,32]{2,1,0:T(8,128)S(1)}, s32[2,8,32]{2,1,0:T(8,128)}, u32[]{:S(2)}) %copy-start.9) | copy-done | bytes 2072
  8.7 0.7 %copy-done.10 = bf16[128,16]{0,1:T(8,128)(2,1)S(1)} copy-done((bf16[128,16]{0,1:T(8,128)(2,1)S(1)}, bf16[128,16]{0,1:T(8,128)(2,1)}, u32[]{:S(2)}) %copy-start.10) | copy-done | bytes 4120
  9.3 0.7 %copy-done.11 = bf16[8,128]{1,0:T(8,128)(2,1)S(1)} copy-done((bf16[8,128]{1,0:T(8,128)(2,1)S(1)}, bf16[8,128]{1,0:T(8,128)(2,1)}, u32[]{:S(2)}) %copy-start.11) | copy-done | bytes 2072
  10.0 0.7 %copy-done.12 = bf16[8,64]{1,0:T(8,128)(2,1)S(1)} copy-done((bf16[8,64]{1,0:T(8,128)(2,1)S(1)}, bf16[8,64]{1,0:T(8,128)(2,1)}, u32[]{:S(2)}) %copy-start.12) | copy-done | bytes 1048
  10.7 0.9 %copy-done.14 = f32[4,16,384]{2,1,0:T(8,128)S(1)} copy-done((f32[4,16,384]{2,1,0:T(8,128)S(1)}, f32[4,16,384]{2,1,0:T(8,128)}, u32[]{:S(2)}) %copy-start.14) | copy-done | bytes 98328
  11.6 0.7 %copy-done.15 = f32[8,256]{1,0:T(8,128)S(1)} copy-done((f32[8,256]{1,0:T(8,128)S(1)}, f32[8,256]{1,0:T(8,128)}, u32[]{:S(2)}) %copy-start.15) | copy-done | bytes 8216
  12.3 23.4 %shard_map.175 = (bf16[512,128]{1,0:T(8,128)(2,1)S(1)}, f32[16,32]{1,0:T(8,128)S(1)}, f32[32,32]{1,0:T(8,128)S(1)}) custom-call(bf16[512,128]{1,0:T(8,128)(2,1)S(1)} %bitcast.17, s32[16,32]{1,0:T(8,128)S(1)} %bitcast.19, s32[16,32]{1,0:T(8,128)S(1)} %bitcast.20, s32[16,32]{1,0:T(8,128)S(1)} %bitcast.21, f32[32,32]{1,0:T(8,128)S(1)} %bitcast.18, ...), custom_call_target="tpu_custom_call" | custom-call | flops 2000000000 | bytes 2000000 | tf_op jit(solution)/shard_map/pallas_call | solution.py:495
  35.7 0.7 %copy.22 = bf16[2,8,32,128]{3,2,1,0:T(8,128)(2,1)} copy(bf16[2,8,32,128]{3,2,1,0:T(8,128)(2,1)S(1)} %bitcast.12) | data formatting | bytes 262144
  36.4 0.6 %copy.23 = f32[2,8,32]{2,1,0:T(8,128)} copy(f32[2,8,32]{2,1,0:T(8,128)S(1)} %bitcast.14) | data formatting | bytes 4096
  37.0 0.6 %copy.24 = f32[2,2,8,32]{3,2,1,0:T(8,128)} copy(f32[2,2,8,32]{3,2,1,0:T(8,128)S(1)} %bitcast.13) | data formatting | bytes 8192
  (12 shorter events, 0.0 us)
Async XLA Ops:
  0.6 0.7 %copy-start.5 = (f32[2,2,8,32]{3,2,1,0:T(8,128)S(1)}, f32[2,2,8,32]{3,2,1,0:T(8,128)}, u32[]{:S(2)}) copy-start(f32[2,2,8,32]{3,2,1,0:T(8,128)} %param.19) | copy-start | bytes 12292
  0.6 0.7 %copy-start.13 = (bf16[128]{0:T(256)(128)(2,1)S(1)}, bf16[128]{0:T(256)(128)(2,1)}, u32[]{:S(2)}) copy-start(bf16[128]{0:T(256)(128)(2,1)} %param.29) | copy-start | bytes 772
  1.4 1.0 %copy-start = (s32[2,8,32,32]{3,2,1,0:T(8,128)S(1)}, s32[2,8,32,32]{3,2,1,0:T(8,128)}, u32[]{:S(2)}) copy-start(s32[2,8,32,32]{3,2,1,0:T(8,128)} %param.20) | copy-start | bytes 196612
  2.3 0.9 %copy-start.1 = (f32[2,8,32,32]{3,2,1,0:T(8,128)S(1)}, f32[2,8,32,32]{3,2,1,0:T(8,128)}, u32[]{:S(2)}) copy-start(f32[2,8,32,32]{3,2,1,0:T(8,128)} %param.22) | copy-start | bytes 196612
  3.3 0.9 %copy-start.2 = (bf16[2,8,32,128]{3,2,1,0:T(8,128)(2,1)S(1)}, bf16[2,8,32,128]{3,2,1,0:T(8,128)(2,1)}, u32[]{:S(2)}) copy-start(bf16[2,8,32,128]{3,2,1,0:T(8,128)(2,1)} %param.16) | copy-start | bytes 393220
  4.2 0.8 %copy-start.3 = (bf16[128,256]{1,0:T(8,128)(2,1)S(1)}, bf16[128,256]{1,0:T(8,128)(2,1)}, u32[]{:S(2)}) copy-start(bf16[128,256]{1,0:T(8,128)(2,1)} %update_in.1) | copy-start | bytes 196612
  5.0 0.8 %copy-start.4 = (bf16[256,128]{1,0:T(8,128)(2,1)S(1)}, bf16[256,128]{1,0:T(8,128)(2,1)}, u32[]{:S(2)}) copy-start(bf16[256,128]{1,0:T(8,128)(2,1)} %update_out.1) | copy-start | bytes 196612
  5.8 0.7 %copy-start.6 = (bf16[64,128]{1,0:T(8,128)(2,1)S(1)}, bf16[64,128]{1,0:T(8,128)(2,1)}, u32[]{:S(2)}) copy-start(bf16[64,128]{1,0:T(8,128)(2,1)} %radial_out.1) | copy-start | bytes 49156
  6.6 0.7 %copy-start.7 = (s32[2,8,32]{2,1,0:T(8,128)S(1)}, s32[2,8,32]{2,1,0:T(8,128)}, u32[]{:S(2)}) copy-start(s32[2,8,32]{2,1,0:T(8,128)} %param.17) | copy-start | bytes 6148
  7.3 0.7 %copy-start.8 = (s32[2,8,32]{2,1,0:T(8,128)S(1)}, s32[2,8,32]{2,1,0:T(8,128)}, u32[]{:S(2)}) copy-start(s32[2,8,32]{2,1,0:T(8,128)} %param.18) | copy-start | bytes 6148
  8.0 0.7 %copy-start.9 = (s32[2,8,32]{2,1,0:T(8,128)S(1)}, s32[2,8,32]{2,1,0:T(8,128)}, u32[]{:S(2)}) copy-start(s32[2,8,32]{2,1,0:T(8,128)} %param.21) | copy-start | bytes 6148
  8.7 0.7 %copy-start.10 = (bf16[128,16]{0,1:T(8,128)(2,1)S(1)}, bf16[128,16]{0,1:T(8,128)(2,1)}, u32[]{:S(2)}) copy-start(bf16[128,16]{0,1:T(8,128)(2,1)} %param.24) | copy-start | bytes 12292
  9.3 0.7 %copy-start.11 = (bf16[8,128]{1,0:T(8,128)(2,1)S(1)}, bf16[8,128]{1,0:T(8,128)(2,1)}, u32[]{:S(2)}) copy-start(bf16[8,128]{1,0:T(8,128)(2,1)} %table.1) | copy-start | bytes 6148
  10.0 0.7 %copy-start.12 = (bf16[8,64]{1,0:T(8,128)(2,1)S(1)}, bf16[8,64]{1,0:T(8,128)(2,1)}, u32[]{:S(2)}) copy-start(bf16[8,64]{1,0:T(8,128)(2,1)} %radial_in.1) | copy-start | bytes 3076
  10.7 0.9 %copy-start.14 = (f32[4,16,384]{2,1,0:T(8,128)S(1)}, f32[4,16,384]{2,1,0:T(8,128)}, u32[]{:S(2)}) copy-start(f32[4,16,384]{2,1,0:T(8,128)} %constant.4.clone.cst) | copy-start | bytes 294916
  11.6 0.7 %copy-start.15 = (f32[8,256]{1,0:T(8,128)S(1)}, f32[8,256]{1,0:T(8,128)}, u32[]{:S(2)}) copy-start(f32[8,256]{1,0:T(8,128)} %constant.5.clone.centers) | copy-start | bytes 24580

commit v3 on v2

--- a/solution.py
+++ b/solution.py
@@ -97,53 +97,73 @@
     return jnp.dot(a, b, preferred_element_type=jnp.float32)
 
 
-def kernel(
-    sizes,
-    feat,
-    species,
-    sublayer,
-    counts,
-    offsets,
-    near,
-    dist,
-    table,
-    charge_w,
-    radial_in,
-    radial_out,
-    update_in,
-    update_out,
-    energy_w,
-    cst,
-    centers,
-    out_feat,
-    out_energy,
-    out_forces,
-    ext,
-    ph,
-    fh,
-    wgt,
-    agg,
-    own_rows,
-    coords,
-    q_all,
-    qw,
-    tb,
-    gz_buf,
-    mine,
-    panel,
-    part,
-    part_buf,
-    send_h,
-    recv_h,
-    send_c,
-    recv_c,
-    send_q,
-    recv_q,
-    send_g,
-    recv_g,
-    send_p,
-    recv_p,
-):
+INPUTS = 16
+
+
+def writer(feat_in, energy_in, forces_in, feat_out, energy_out, forces_out, sems):
+    pairs = ((feat_in, feat_out), (energy_in, energy_out), (forces_in, forces_out))
+    copies = [pltpu.make_async_copy(a, b, sems.at[i]) for i, (a, b) in enumerate(pairs)]
+    for copy in copies:
+        copy.start()
+    for copy in copies:
+        copy.wait()
+
+
+def kernel(sizes, *refs):
+    in_hbm, refs = refs[:INPUTS], refs[INPUTS:]
+    (out_feat, out_energy, out_forces), refs = refs[:3], refs[3:]
+    held, refs = refs[:INPUTS], refs[INPUTS:]
+    (
+        load_sem,
+        ext,
+        ph,
+        fh,
+        wgt,
+        agg,
+        own_rows,
+        coords,
+        q_all,
+        qw,
+        tb,
+        gz_buf,
+        mine,
+        panel,
+        part,
+        part_buf,
+        send_h,
+        recv_h,
+        send_c,
+        recv_c,
+        send_q,
+        recv_q,
+        send_g,
+        recv_g,
+        send_p,
+        recv_p,
+    ) = refs
+    (
+        species,
+        sublayer,
+        counts,
+        offsets,
+        feat,
+        table,
+        charge_w,
+        cst,
+        dist,
+        near,
+        centers,
+        radial_in,
+        radial_out,
+        update_in,
+        update_out,
+        energy_w,
+    ) = held
+    loads = [
+        pltpu.make_async_copy(a, b, load_sem.at[i]) for i, (a, b) in enumerate(zip(in_hbm, held))
+    ]
+    for load in loads:
+        load.start()
     zc, xc, slots, entries, channels, n_xy, n_gz = sizes
     cells = zc * xc
     atoms = cells * slots
@@ -175,6 +195,8 @@
                     barrier, inc=1, device_id={"gz": gz + step, "xy": side}, device_id_type=MESH
                 )
 
+    for load in loads[:4]:
+        load.wait()
     unfold = (iota(i32, (slots, atoms), 1) % slots == iota(i32, (slots, atoms), 0)).astype(f32)
     own_cell = iota(i32, (cells, atoms), 1) // slots == iota(i32, (cells, atoms), 0)
     stacked = jnp.concatenate(
@@ -194,6 +216,8 @@
     coords[xy] = rows
     cols = jnp.transpose(rows)
 
+    for load in loads[4:7]:
+        load.wait()
     kinds = table.shape[0]
     onehot = cols[:, 3:4] == iota(i32, (atoms, kinds), 1).astype(f32)
     hidden = (feat[...].astype(f32) + dot(onehot.astype(f32).astype(bf16), table[...])).astype(bf16)
@@ -284,9 +308,12 @@
         qw[strip] = weighted
         return dot(weighted, ph[pl.ds(strip * atoms, atoms), :])
 
+    loads[7].wait()
     strip_phases(xy)
     total = strip_moments(xy)
 
+    for load in loads[8:]:
+        load.wait()
     d_all = dist[...]
     slot = iota(i32, (atoms, 1), 0) % slots
     entry = iota(i32, (atoms, entries), 1)
@@ -359,16 +386,20 @@
         for copy in down:
             copy.wait_recv()
 
-    codes = iota(i32, (slots, 9 * slots), 1)
+    half = 9 * slots // 2
+    codes = iota(i32, (slots, half), 1)
 
     def edge_row(z):
         def one(x, carry):
             base = pl.multiple_of((z * xc + x) * slots, slots)
             region = ext[z : z + 3, pl.ds(x, 3)].reshape(9 * slots, width)
+            region = jnp.concatenate([region[:half], region[half:]], axis=1)
             index = near[pl.ds(base, slots), :]
+            upper = jnp.where(index >= half, 1, 0)
+            folded = index - half * upper
             chosen = jnp.concatenate(
                 [
-                    jnp.where(index[:, e : e + 1] == codes, 1.0, 0.0).astype(bf16)
+                    jnp.where(folded[:, e : e + 1] == codes, 1.0, 0.0).astype(bf16)
                     for e in range(entries)
                 ],
                 axis=0,
@@ -384,7 +415,9 @@
             for e in range(entries):
                 row, col = (e // pack) * slots, (e % pack) * width
                 filtered = weight[:, e : e + 1] * filters[row : row + slots, col : col + width]
-                acc = acc + filtered * gathered[e * slots : (e + 1) * slots]
+                pair = gathered[e * slots : (e + 1) * slots]
+                rows_of = jnp.where(upper[:, e : e + 1] == 1, pair[:, width:], pair[:, :width])
+                acc = acc + filtered * rows_of
             agg[pl.ds(base, slots), :] = acc.astype(bf16)
             return carry
 
@@ -492,16 +525,38 @@
     sizes = (zc, xc, slots, entries, channels, n_xy, n_gz)
     dma = pltpu.SemaphoreType.DMA
     vmem = pl.BlockSpec(memory_space=pltpu.VMEM)
-    out_feat, energy, forces = pl.pallas_call(
+    operands = (
+        species.reshape(cells, slots),
+        sublayer.reshape(cells, slots),
+        neighbour_count.reshape(cells, slots),
+        offsets.reshape(2 * cells, slots),
+        features.reshape(atoms, width),
+        species_table,
+        charge_weight.T,
+        jnp.asarray(cst),
+        distances.reshape(atoms, entries),
+        neighbours.reshape(atoms, entries),
+        jnp.asarray(centers),
+        radial_in,
+        radial_out,
+        update_in,
+        update_out,
+        energy_weight.reshape(1, width),
+    )
+    hbm = pl.BlockSpec(memory_space=pltpu.HBM)
+    shapes = (
+        jax.ShapeDtypeStruct((atoms, width), bf16),
+        jax.ShapeDtypeStruct((cells, slots), f32),
+        jax.ShapeDtypeStruct((2 * cells, slots), f32),
+    )
+    results = pl.pallas_call(
         functools.partial(kernel, sizes),
-        out_shape=(
-            jax.ShapeDtypeStruct((atoms, width), bf16),
-            jax.ShapeDtypeStruct((cells, slots), f32),
-            jax.ShapeDtypeStruct((2 * cells, slots), f32),
-        ),
-        in_specs=[vmem] * 16,
+        out_shape=shapes,
+        in_specs=[hbm] * INPUTS,
         out_specs=(vmem, vmem, vmem),
-        scratch_shapes=[
+        scratch_shapes=[pltpu.VMEM(a.shape, a.dtype) for a in operands]
+        + [
+            dma((INPUTS,)),
             pltpu.VMEM((zc + 2, xc + 2, slots, width), bf16),
             pltpu.VMEM((n_xy * atoms, LANES), bf16),
             pltpu.VMEM((atoms, entries * radial), bf16),
@@ -529,27 +584,17 @@
             dma((n_xy - 1,)),
         ],
         compiler_params=pltpu.CompilerParams(
-            collective_id=0, has_side_effects=True, vmem_limit_bytes=40 * 1024 * 1024
+            collective_id=0, has_side_effects=True, vmem_limit_bytes=60 * 1024 * 1024
         ),
         cost_estimate=pl.CostEstimate(flops=2_000_000_000, bytes_accessed=2_000_000, transcendentals=2_000_000),
-    )(
-        features.reshape(atoms, width),
-        species.reshape(cells, slots),
-        sublayer.reshape(cells, slots),
-        neighbour_count.reshape(cells, slots),
-        offsets.reshape(2 * cells, slots),
-        neighbours.reshape(atoms, entries),
-        distances.reshape(atoms, entries),
-        species_table,
-        charge_weight.T,
-        radial_in,
-        radial_out,
-        update_in,
-        update_out,
-        energy_weight.reshape(1, width),
-        jnp.asarray(cst),
-        jnp.asarray(centers),
-    )
+    )(*operands)
+    out_feat, energy, forces = pl.pallas_call(
+        writer,
+        out_shape=shapes,
+        in_specs=[vmem] * 3,
+        out_specs=(hbm, hbm, hbm),
+        scratch_shapes=[dma((3,))],
+    )(*results)
     return (
         out_feat.reshape(features.shape),
         energy.reshape(species.shape),

time: 38.2 us -> 27.7 us (0.73)
  the two profiles are of different devices: /device:TPU:1 before, /device:TPU:0 now
where the time goes in v3:
time: 27.7 us; the launch traced here: 27.3 us
  Pallas kernels  26.7 us (96%)
  between operations  0.64 us (2%)
    pallas_call x1, Pallas kernels, shards(): pl.pallas_call(functools.partial(kernel, sizes), out_shape=shapes, in_spe...  25.1 us
    pallas_call x1, Pallas kernels, shards(): pl.pallas_call(writer, out_shape=shapes, in_specs=[vmem] * 3, out_specs=(...  1.61 us

profile of v3, /device:TPU:0, one launch (start us, length us, event | category | flops | bytes accessed | tf_op | source)
XLA Modules:
  0.0 27.3 jit_solution(180818759941987541)
XLA Ops:
  0.6 25.1 %shard_map.175 = (bf16[512,128]{1,0:T(8,128)(2,1)}, f32[16,32]{1,0:T(8,128)}, f32[32,32]{1,0:T(8,128)}) custom-call(s32[16,32]{1,0:T(8,128)} %bitcast.18, s32[16,32]{1,0:T(8,128)} %bitcast.19, s32[16,32]{1,0:T(8,128)} %bitcast.20, f32[32,32]{1,0:T(8,128)} %bitcast.16, bf16[512,128]{1,0:T(8,128)(2,1)} %bitcast.14, bf16[8,128]{1,0:T(8,128)(2,1)} %refs_5_.1, ...), custom_call_target="tpu_custom_call" | custom-call | flops 2000000000 | bytes 2000000 | tf_op jit(solution)/shard_map/pallas_call | solution.py:552
  25.7 1.6 %shard_map.176 = (bf16[512,128]{1,0:T(8,128)(2,1)}, f32[16,32]{1,0:T(8,128)}, f32[32,32]{1,0:T(8,128)}) custom-call(bf16[512,128]{1,0:T(8,128)(2,1)} %get-tuple-element.9.feat_in, f32[16,32]{1,0:T(8,128)} %get-tuple-element.10.energy_in, f32[32,32]{1,0:T(8,128)} %get-tuple-element.11.forces_in), custom_call_target="tpu_custom_call" | custom-call | tf_op jit(solution)/shard_map/pallas_call | solution.py:591

commit v4 on v3

--- a/solution.py
+++ b/solution.py
@@ -36,7 +36,9 @@
         weight = f32(coupling * (2.0 * math.pi / (width_x * cell_width))) * np.exp(
             f32(-0.5 * smearing * smearing) * square
         )
-        return wave_x, wave_y, weight / screened * count, screened
+        quarter_x = (4.0 / width_x * (index_x - KX // 2)).astype(f32)
+        quarter_y = (4.0 / cell_width * (index_y - KY // 2)).astype(f32)
+        return wave_x, wave_y, weight / screened * count, screened, quarter_x, quarter_y
 
     strips = []
     for strip in range(n_xy):
@@ -57,30 +59,32 @@
         lanes = []
         for one, two in zip(part_a, part_b):
             one = np.pad(one, (0, 128 - one.size))
-            two = np.pad(two, (0, 64 - two.size))
-            lanes.append(np.concatenate([one, one, two, two]))
-        wave_x, wave_y, weight, screened = lanes
-        sign = np.repeat(np.array([1, -1, 1, -1], f32), [128, 128, 64, 64])
+            two = np.pad(two, (0, 32 - two.size))
+            lanes.append(np.concatenate([one, one, two, two, two, two]))
+        wave_x, wave_y, weight, screened, *quarters = lanes
+        sign = np.repeat(np.array([1, -1, 1, -1, 1, -1], f32), [128, 128, 32, 32, 32, 32])
         powers = [np.exp(-screened * f32(layer_depth) * f32(n)) for n in range(layers + 1)]
-        rows = [wave_x, wave_y, weight, sign * wave_x, sign * wave_y] + powers
+        rows = [*quarters, weight, sign * wave_x, sign * wave_y] + powers
         rows += [np.zeros(LANES, f32)] * (-len(rows) % 8)
         strips.append(np.stack(rows))
     return np.stack(strips).astype(f32)
 
 
-def reduced(angle):
-    turns = jnp.floor(angle * (2.0 / math.pi) + 0.5)
-    rest = angle - turns * 1.5703125
-    rest = rest - turns * 4.8375129699707031e-4
-    rest = rest - turns * 7.5497899548918822e-8
+def reduced(quarters):
+    whole = (quarters + 12582912.0) - 12582912.0
+    rest = quarters - whole
     square = rest * rest
-    sine = rest + rest * square * (
-        (-1.9515295891e-4 * square + 8.3321608736e-3) * square - 1.6666654611e-1
-    )
-    cosine = (1.0 - 0.5 * square) + square * square * (
-        (2.443315711809948e-5 * square - 1.388731625493765e-3) * square + 4.166664568298827e-2
-    )
-    return turns.astype(jnp.int32), sine, cosine
+    q = math.pi / 2.0
+    sine = rest * (
+        (((-1.9515295891e-4 * q**7) * square + 8.3321608736e-3 * q**5) * square - 1.6666654611e-1 * q**3)
+        * square
+        + q
+    )
+    cosine = (
+        (((2.443315711809948e-5 * q**8) * square - 1.388731625493765e-3 * q**6) * square
+         + 4.166664568298827e-2 * q**4) * square - 0.5 * q**2
+    ) * square + 1.0
+    return whole.astype(jnp.int32), sine, cosine
 
 
 def at_quadrant(quadrant, sine, cosine):
@@ -287,17 +291,25 @@
 
     def strip_phases(strip):
         at = jnp.transpose(coords[strip])
-        turn = jnp.where(iota(i32, (1, 128), 1) < 64, 1, 0)
+        lane = iota(i32, (1, 128), 1)
+        turn = jnp.where(lane % 64 < 32, 1, 0)
+        first = lane < 64
         step = 64
-        for start in range(0, atoms, step):
-            here = slice(start, start + step)
-            at_x, at_y = at[here, 0:1], at[here, 1:2]
-            lines = pl.ds(strip * atoms + start, step)
-            quadrant, sine, cosine = reduced(at_x * cst[xy, 0:1, :128] + at_y * cst[xy, 1:2, :128])
-            ph[lines, :128] = at_quadrant(quadrant + 1, sine, cosine).astype(bf16)
-            ph[lines, 128:256] = at_quadrant(quadrant, sine, cosine).astype(bf16)
-            quadrant, sine, cosine = reduced(at_x * cst[xy, 0:1, 256:] + at_y * cst[xy, 1:2, 256:])
-            ph[lines, 256:] = at_quadrant(quadrant + turn, sine, cosine).astype(bf16)
+        for start in range(0, atoms // 2, step):
+            value = []
+            for part in range(2):
+                row = start + part * (atoms // 2)
+                at_x, at_y = at[row : row + step, 0:1], at[row : row + step, 1:2]
+                lines = pl.ds(strip * atoms + row, step)
+                quadrant, sine, cosine = reduced(at_x * cst[xy, 0:1, :128] + at_y * cst[xy, 1:2, :128])
+                ph[lines, :128] = at_quadrant(quadrant + 1, sine, cosine).astype(bf16)
+                ph[lines, 128:256] = at_quadrant(quadrant, sine, cosine).astype(bf16)
+                value.append(at_x * cst[xy, 0:1, 256:] + at_y * cst[xy, 1:2, 256:])
+            quadrant, sine, cosine = reduced(jnp.where(first, value[0], value[1]))
+            both = at_quadrant(quadrant + turn, sine, cosine)
+            for part in range(2):
+                lines = pl.ds(strip * atoms + start + part * (atoms // 2), step)
+                ph[lines, 256:] = jnp.where(first == (part == 0), both, 0.0).astype(bf16)
 
     def strip_moments(strip):
         layer = coords[strip][2:3]
@@ -352,7 +364,9 @@
         return total + strip_moments(strip)
 
     total = lax.fori_loop(1, n_xy, add_strip, total)
-    mine[...] = total
+    spare = total[:, 256:]
+    mine[:, :256] = total[:, :256]
+    mine[:, 256:] = spare + jnp.concatenate([spare[:, 64:], spare[:, :64]], axis=1)
 
     def power(n):
         return cst[xy, 5 + n : 6 + n, :]
@@ -387,7 +401,8 @@
             copy.wait_recv()
 
     half = 9 * slots // 2
-    codes = iota(i32, (slots, half), 1)
+    codes = iota(i32, (slots, half), 1).astype(f32).astype(bf16)
+    hit, miss = jnp.ones(codes.shape, bf16), jnp.zeros(codes.shape, bf16)
 
     def edge_row(z):
         def one(x, carry):
@@ -395,14 +410,12 @@
             region = ext[z : z + 3, pl.ds(x, 3)].reshape(9 * slots, width)
             region = jnp.concatenate([region[:half], region[half:]], axis=1)
             index = near[pl.ds(base, slots), :]
-            upper = jnp.where(index >= half, 1, 0)
-            folded = index - half * upper
+            upper = index >= half
+            folded = jnp.where(upper, index - half, index).astype(f32).astype(bf16)
+            weight = wgt[pl.ds(base, slots), :]
+            signed = jnp.where(upper, -weight, weight)
             chosen = jnp.concatenate(
-                [
-                    jnp.where(folded[:, e : e + 1] == codes, 1.0, 0.0).astype(bf16)
-                    for e in range(entries)
-                ],
-                axis=0,
+                [jnp.where(folded[:, e : e + 1] == codes, hit, miss) for e in range(entries)], axis=0
             )
             gathered = dot(chosen, region)
             hid = fh[pl.ds(base, slots), :]
@@ -410,18 +423,18 @@
                 [hid[:, p * 128 : (p + 1) * 128] for p in range(hid.shape[1] // 128)], axis=0
             )
             filters = dot(both, hidden_out)
-            weight = wgt[pl.ds(base, slots), :]
             acc = jnp.zeros((slots, width), f32)
             for e in range(entries):
                 row, col = (e // pack) * slots, (e % pack) * width
-                filtered = weight[:, e : e + 1] * filters[row : row + slots, col : col + width]
+                mark = jnp.broadcast_to(signed[:, e : e + 1], (slots, width))
+                filtered = jnp.abs(mark) * filters[row : row + slots, col : col + width]
                 pair = gathered[e * slots : (e + 1) * slots]
-                rows_of = jnp.where(upper[:, e : e + 1] == 1, pair[:, width:], pair[:, :width])
+                rows_of = jnp.where(mark < 0.0, pair[:, width:], pair[:, :width])
                 acc = acc + filtered * rows_of
             agg[pl.ds(base, slots), :] = acc.astype(bf16)
             return carry
 
-        lax.fori_loop(0, xc, one, 0)
+        lax.fori_loop(0, xc, one, 0, unroll=2)
 
     for z in range(zc // 2):
         edge_row(z)
@@ -438,7 +451,9 @@
             value = value + power(abs(l - m)) * layer_moments(m)
         value = value * cst[xy, 2:3, :]
         swapped = jnp.concatenate(
-            [value[:, 128:256], value[:, :128], value[:, 320:], value[:, 256:320]], axis=1
+            [value[:, 128:256], value[:, :128]]
+            + [value[:, 256 + 32 * n : 288 + 32 * n] for n in (1, 0, 3, 2)],
+            axis=1,
         )
         lines = (value, cst[xy, 3:4, :] * swapped, cst[xy, 4:5, :] * swapped)
         for r, line in enumerate(lines):

time: 27.7 us -> 24.6 us (0.89)
  Pallas kernels: 26.7 us -> 23.8 us
    pallas_call x1, Pallas kernels: 25.1 us -> 22.2 us  [shards(): pl.pallas_call(functools.partial(kernel, sizes), out_shape=shapes, in_spe...]
where the time goes in v4:
time: 24.6 us; the launch traced here: 24.4 us
  Pallas kernels  23.8 us (97%)
  between operations  0.64 us (3%)
    pallas_call x1, Pallas kernels, shards(): pl.pallas_call(functools.partial(kernel, sizes), out_shape=shapes, in_spe...  22.2 us
    pallas_call x1, Pallas kernels, shards(): pl.pallas_call(writer, out_shape=shapes, in_specs=[vmem] * 3, out_specs=(...  1.61 us

profile of v4, /device:TPU:0, one launch (start us, length us, event | category | flops | bytes accessed | tf_op | source)
XLA Modules:
  0.0 24.4 jit_solution(6739552355144270878)
XLA Ops:
  0.6 22.2 %shard_map.175 = (bf16[512,128]{1,0:T(8,128)(2,1)}, f32[16,32]{1,0:T(8,128)}, f32[32,32]{1,0:T(8,128)}) custom-call(s32[16,32]{1,0:T(8,128)} %bitcast.18, s32[16,32]{1,0:T(8,128)} %bitcast.19, s32[16,32]{1,0:T(8,128)} %bitcast.20, f32[32,32]{1,0:T(8,128)} %bitcast.16, bf16[512,128]{1,0:T(8,128)(2,1)} %bitcast.14, bf16[8,128]{1,0:T(8,128)(2,1)} %refs_5_.1, ...), custom_call_target="tpu_custom_call" | custom-call | flops 2000000000 | bytes 2000000 | tf_op jit(solution)/shard_map/pallas_call | solution.py:567
  22.8 1.6 %shard_map.176 = (bf16[512,128]{1,0:T(8,128)(2,1)}, f32[16,32]{1,0:T(8,128)}, f32[32,32]{1,0:T(8,128)}) custom-call(bf16[512,128]{1,0:T(8,128)(2,1)} %get-tuple-element.9.feat_in, f32[16,32]{1,0:T(8,128)} %get-tuple-element.10.energy_in, f32[32,32]{1,0:T(8,128)} %get-tuple-element.11.forces_in), custom_call_target="tpu_custom_call" | custom-call | tf_op jit(solution)/shard_map/pallas_call | solution.py:606

commit v5 on v4

--- a/solution.py
+++ b/solution.py
@@ -238,57 +238,6 @@
     def _():
         ext[zc + 1] = jnp.zeros(ext.shape[1:], bf16)
 
-    diagonals = 2 * (has_below.astype(i32) + has_above.astype(i32))
-    pl.semaphore_wait(barrier, n_xy - 1 + n_gz - 1 + diagonals)
-
-    def remote(src, dst, send, recv, target):
-        return pltpu.make_async_remote_copy(
-            src_ref=src,
-            dst_ref=dst,
-            send_sem=send,
-            recv_sem=recv,
-            device_id=target,
-            device_id_type=MESH,
-        )
-
-    strip_copies = []
-    for d, peer in enumerate(xy_peers):
-        strip_copies += [
-            remote(coords.at[xy], coords.at[xy], send_c.at[d], recv_c.at[d], {"xy": peer}),
-            remote(q_all.at[xy], q_all.at[xy], send_q.at[d], recv_q.at[d], {"xy": peer}),
-        ]
-    for copy in strip_copies:
-        copy.start()
-
-    inner = pl.ds(1, zc)
-    x_copies = [
-        remote(ext.at[inner, 1], ext.at[inner, xc + 1], send_h.at[0], recv_h.at[0], {"xy": left}),
-        remote(ext.at[inner, xc], ext.at[inner, 0], send_h.at[1], recv_h.at[1], {"xy": right}),
-    ]
-
-    def z_copies(first, own, ghost, target):
-        strip = pl.ds(1, xc)
-        return [
-            remote(ext.at[own, strip], ext.at[ghost, strip], send_h.at[first], recv_h.at[first], {"gz": target}),
-            remote(ext.at[own, 1], ext.at[ghost, xc + 1], send_h.at[first + 1], recv_h.at[first + 1], {"gz": target, "xy": left}),
-            remote(ext.at[own, xc], ext.at[ghost, 0], send_h.at[first + 2], recv_h.at[first + 2], {"gz": target, "xy": right}),
-        ]
-
-    down = z_copies(2, 1, zc + 1, gz - 1)
-    rise = z_copies(5, zc, 0, gz + 1)
-    for copy in x_copies:
-        copy.start()
-
-    @pl.when(has_below)
-    def _():
-        for copy in down:
-            copy.start()
-
-    @pl.when(has_above)
-    def _():
-        for copy in rise:
-            copy.start()
-
     def strip_phases(strip):
         at = jnp.transpose(coords[strip])
         lane = iota(i32, (1, 128), 1)
@@ -336,9 +285,67 @@
     basis_count, radial = radial_in.shape
     spread_shape = (entries, entries * basis_count)
     spread = (iota(i32, spread_shape, 1) // basis_count == iota(i32, spread_shape, 0)).astype(f32)
-    spacing = jnp.dot(d_all, spread, precision=exact, preferred_element_type=f32)
+    d_high = d_all.astype(bf16)
+    d_rest = d_all - d_high.astype(f32)
+    d_mid = d_rest.astype(bf16)
+    d_low = (d_rest - d_mid.astype(f32)).astype(bf16)
+    spread = jnp.concatenate([spread] * 3, axis=0).astype(bf16)
+    spacing = dot(jnp.concatenate([d_high, d_mid, d_low], axis=1), spread)
     gap = spacing - centers[0:1, :]
     basis = jnp.exp(-(gap * gap)).astype(bf16)
+
+    diagonals = 2 * (has_below.astype(i32) + has_above.astype(i32))
+    pl.semaphore_wait(barrier, n_xy - 1 + n_gz - 1 + diagonals)
+
+    def remote(src, dst, send, recv, target):
+        return pltpu.make_async_remote_copy(
+            src_ref=src,
+            dst_ref=dst,
+            send_sem=send,
+            recv_sem=recv,
+            device_id=target,
+            device_id_type=MESH,
+        )
+
+    strip_copies = []
+    for d, peer in enumerate(xy_peers):
+        strip_copies += [
+            remote(coords.at[xy], coords.at[xy], send_c.at[d], recv_c.at[d], {"xy": peer}),
+            remote(q_all.at[xy], q_all.at[xy], send_q.at[d], recv_q.at[d], {"xy": peer}),
+        ]
+    for copy in strip_copies:
+        copy.start()
+
+    inner = pl.ds(1, zc)
+    x_copies = [
+        remote(ext.at[inner, 1], ext.at[inner, xc + 1], send_h.at[0], recv_h.at[0], {"xy": left}),
+        remote(ext.at[inner, xc], ext.at[inner, 0], send_h.at[1], recv_h.at[1], {"xy": right}),
+    ]
+
+    def z_copies(first, own, ghost, target):
+        strip = pl.ds(1, xc)
+        return [
+            remote(ext.at[own, strip], ext.at[ghost, strip], send_h.at[first], recv_h.at[first], {"gz": target}),
+            remote(ext.at[own, 1], ext.at[ghost, xc + 1], send_h.at[first + 1], recv_h.at[first + 1], {"gz": target, "xy": left}),
+            remote(ext.at[own, xc], ext.at[ghost, 0], send_h.at[first + 2], recv_h.at[first + 2], {"gz": target, "xy": right}),
+        ]
+
+    down = z_copies(2, 1, zc + 1, gz - 1)
+    rise = z_copies(5, zc, 0, gz + 1)
+    for copy in x_copies:
+        copy.start()
+
+    @pl.when(has_below)
+    def _():
+        for copy in down:
+            copy.start()
+
+    @pl.when(has_above)
+    def _():
+        for copy in rise:
+            copy.start()
+
+
     group = 128 // basis_count
     tall = jnp.concatenate([radial_in[...].astype(f32)] * group, axis=0)
     flat = jnp.concatenate([tall] * group, axis=1)
@@ -363,7 +370,7 @@
         strip_phases(strip)
         return total + strip_moments(strip)
 
-    total = lax.fori_loop(1, n_xy, add_strip, total)
+    total = lax.fori_loop(1, n_xy, add_strip, total, unroll=3)
     spare = total[:, 256:]
     mine[:, :256] = total[:, :256]
     mine[:, 256:] = spare + jnp.concatenate([spare[:, 64:], spare[:, :64]], axis=1)
@@ -434,7 +441,7 @@
             agg[pl.ds(base, slots), :] = acc.astype(bf16)
             return carry
 
-        lax.fori_loop(0, xc, one, 0, unroll=2)
+        lax.fori_loop(0, xc, one, 0, unroll=4)
 
     for z in range(zc // 2):
         edge_row(z)

time: 24.6 us -> 24.2 us (0.984)
  Pallas kernels: 23.8 us -> 23.3 us
    pallas_call x1, Pallas kernels: 22.2 us -> 21.7 us  [shards(): pl.pallas_call(functools.partial(kernel, sizes), out_shape=shapes, in_spe...]
where the time goes in v5:
time: 24.2 us; the launch traced here: 24 us
  Pallas kernels  23.3 us (96%)
  between operations  0.64 us (3%)
    pallas_call x1, Pallas kernels, shards(): pl.pallas_call(functools.partial(kernel, sizes), out_shape=shapes, in_spe...  21.7 us
    pallas_call x1, Pallas kernels, shards(): pl.pallas_call(writer, out_shape=shapes, in_specs=[vmem] * 3, out_specs=(...  1.61 us

profile of v5, /device:TPU:0, one launch (start us, length us, event | category | flops | bytes accessed | tf_op | source)
XLA Modules:
  0.0 24.0 jit_solution(8066841211274735053)
XLA Ops:
  0.6 21.7 %shard_map.175 = (bf16[512,128]{1,0:T(8,128)(2,1)}, f32[16,32]{1,0:T(8,128)}, f32[32,32]{1,0:T(8,128)}) custom-call(s32[16,32]{1,0:T(8,128)} %bitcast.18, s32[16,32]{1,0:T(8,128)} %bitcast.19, s32[16,32]{1,0:T(8,128)} %bitcast.20, f32[32,32]{1,0:T(8,128)} %bitcast.16, bf16[512,128]{1,0:T(8,128)(2,1)} %bitcast.14, bf16[8,128]{1,0:T(8,128)(2,1)} %refs_5_.1, ...), custom_call_target="tpu_custom_call" | custom-call | flops 2000000000 | bytes 2000000 | tf_op jit(solution)/shard_map/pallas_call | solution.py:574
  22.3 1.6 %shard_map.176 = (bf16[512,128]{1,0:T(8,128)(2,1)}, f32[16,32]{1,0:T(8,128)}, f32[32,32]{1,0:T(8,128)}) custom-call(bf16[512,128]{1,0:T(8,128)(2,1)} %get-tuple-element.9.feat_in, f32[16,32]{1,0:T(8,128)} %get-tuple-element.10.energy_in, f32[32,32]{1,0:T(8,128)} %get-tuple-element.11.forces_in), custom_call_target="tpu_custom_call" | custom-call | tf_op jit(solution)/shard_map/pallas_call | solution.py:613

commit v6 on v5

--- a/solution.py
+++ b/solution.py
@@ -60,9 +60,9 @@
         for one, two in zip(part_a, part_b):
             one = np.pad(one, (0, 128 - one.size))
             two = np.pad(two, (0, 32 - two.size))
-            lanes.append(np.concatenate([one, one, two, two, two, two]))
+            lanes.append(np.concatenate([one, one, two, two, np.zeros(64)]).astype(f32))
         wave_x, wave_y, weight, screened, *quarters = lanes
-        sign = np.repeat(np.array([1, -1, 1, -1, 1, -1], f32), [128, 128, 32, 32, 32, 32])
+        sign = np.repeat(np.array([1, -1, 1, -1, 0], f32), [128, 128, 32, 32, 64])
         powers = [np.exp(-screened * f32(layer_depth) * f32(n)) for n in range(layers + 1)]
         rows = [*quarters, weight, sign * wave_x, sign * wave_y] + powers
         rows += [np.zeros(LANES, f32)] * (-len(rows) % 8)
@@ -239,26 +239,17 @@
         ext[zc + 1] = jnp.zeros(ext.shape[1:], bf16)
 
     def strip_phases(strip):
-        at = jnp.transpose(coords[strip])
-        lane = iota(i32, (1, 128), 1)
-        turn = jnp.where(lane % 64 < 32, 1, 0)
-        first = lane < 64
-        step = 64
-        for start in range(0, atoms // 2, step):
-            value = []
-            for part in range(2):
-                row = start + part * (atoms // 2)
-                at_x, at_y = at[row : row + step, 0:1], at[row : row + step, 1:2]
-                lines = pl.ds(strip * atoms + row, step)
-                quadrant, sine, cosine = reduced(at_x * cst[xy, 0:1, :128] + at_y * cst[xy, 1:2, :128])
-                ph[lines, :128] = at_quadrant(quadrant + 1, sine, cosine).astype(bf16)
-                ph[lines, 128:256] = at_quadrant(quadrant, sine, cosine).astype(bf16)
-                value.append(at_x * cst[xy, 0:1, 256:] + at_y * cst[xy, 1:2, 256:])
-            quadrant, sine, cosine = reduced(jnp.where(first, value[0], value[1]))
-            both = at_quadrant(quadrant + turn, sine, cosine)
-            for part in range(2):
-                lines = pl.ds(strip * atoms + start + part * (atoms // 2), step)
-                ph[lines, 256:] = jnp.where(first == (part == 0), both, 0.0).astype(bf16)
+        at_x, at_y = coords[strip][0:1], coords[strip][1:2]
+        step = 32
+        for start in range(0, 128, step):
+            here = slice(start, start + step)
+            quadrant, sine, cosine = reduced(waves[here, 0:1] * at_x + waves[here, 1:2] * at_y)
+            ph[strip, start : start + step] = at_quadrant(quadrant + 1, sine, cosine).astype(bf16)
+            ph[strip, 128 + start : 128 + start + step] = at_quadrant(quadrant, sine, cosine).astype(bf16)
+        quadrant, sine, cosine = reduced(waves[256:288, 0:1] * at_x + waves[256:288, 1:2] * at_y)
+        ph[strip, 256:288] = at_quadrant(quadrant + 1, sine, cosine).astype(bf16)
+        ph[strip, 288:320] = at_quadrant(quadrant, sine, cosine).astype(bf16)
+        ph[strip, 320:] = jnp.zeros((LANES - 320, atoms), bf16)
 
     def strip_moments(strip):
         layer = coords[strip][2:3]
@@ -267,9 +258,12 @@
             [jnp.where(layer == float(l), charges, 0.0) for l in range(layers)], axis=0
         ).astype(bf16)
         qw[strip] = weighted
-        return dot(weighted, ph[pl.ds(strip * atoms, atoms), :])
+        return lax.dot_general(
+            ph[strip], weighted, (((1,), (1,)), ((), ())), preferred_element_type=f32
+        )
 
     loads[7].wait()
+    waves = jnp.transpose(cst[xy, 0:8, :])
     strip_phases(xy)
     total = strip_moments(xy)
 
@@ -371,9 +365,7 @@
         return total + strip_moments(strip)
 
     total = lax.fori_loop(1, n_xy, add_strip, total, unroll=3)
-    spare = total[:, 256:]
-    mine[:, :256] = total[:, :256]
-    mine[:, 256:] = spare + jnp.concatenate([spare[:, 64:], spare[:, :64]], axis=1)
+    mine[...] = jnp.transpose(total)
 
     def power(n):
         return cst[xy, 5 + n : 6 + n, :]
@@ -459,7 +451,7 @@
         value = value * cst[xy, 2:3, :]
         swapped = jnp.concatenate(
             [value[:, 128:256], value[:, :128]]
-            + [value[:, 256 + 32 * n : 288 + 32 * n] for n in (1, 0, 3, 2)],
+            + [value[:, 288:320], value[:, 256:288], value[:, 320:]],
             axis=1,
         )
         lines = (value, cst[xy, 3:4, :] * swapped, cst[xy, 4:5, :] * swapped)
@@ -468,12 +460,7 @@
             panel[top : top + channels, :] = line.astype(bf16)
 
     def strip_sums(strip):
-        evaluated = lax.dot_general(
-            panel[...],
-            ph[pl.ds(strip * atoms, atoms), :],
-            (((1,), (1,)), ((), ())),
-            preferred_element_type=f32,
-        )
+        evaluated = dot(panel[...], ph[strip])
         charges = qw[strip].astype(f32)
         lines = [
             jnp.sum(evaluated[r * pairs : (r + 1) * pairs] * charges, axis=0, keepdims=True)
@@ -580,7 +567,7 @@
         + [
             dma((INPUTS,)),
             pltpu.VMEM((zc + 2, xc + 2, slots, width), bf16),
-            pltpu.VMEM((n_xy * atoms, LANES), bf16),
+            pltpu.VMEM((n_xy, LANES, atoms), bf16),
             pltpu.VMEM((atoms, entries * radial), bf16),
             pltpu.VMEM((atoms, entries), f32),
             pltpu.VMEM((atoms, width), bf16),

time: 24.2 us -> 23.8 us (0.983)
  Pallas kernels: 23.3 us -> 22.9 us
    pallas_call x1, Pallas kernels: 21.7 us -> 21.3 us  [shards(): pl.pallas_call(functools.partial(kernel, sizes), out_shape=shapes, in_spe...]
where the time goes in v6:
time: 23.8 us; the launch traced here: 23.6 us
  Pallas kernels  22.9 us (96%)
  between operations  0.64 us (3%)
    pallas_call x1, Pallas kernels, shards(): pl.pallas_call(functools.partial(kernel, sizes), out_shape=shapes, in_spe...  21.3 us
    pallas_call x1, Pallas kernels, shards(): pl.pallas_call(writer, out_shape=shapes, in_specs=[vmem] * 3, out_specs=(...  1.61 us

profile of v6, /device:TPU:0, one launch (start us, length us, event | category | flops | bytes accessed | tf_op | source)
XLA Modules:
  0.0 23.6 jit_solution(17279649185467315566)
XLA Ops:
  0.6 21.3 %shard_map.175 = (bf16[512,128]{1,0:T(8,128)(2,1)}, f32[16,32]{1,0:T(8,128)}, f32[32,32]{1,0:T(8,128)}) custom-call(s32[16,32]{1,0:T(8,128)} %bitcast.18, s32[16,32]{1,0:T(8,128)} %bitcast.19, s32[16,32]{1,0:T(8,128)} %bitcast.20, f32[32,32]{1,0:T(8,128)} %bitcast.16, bf16[512,128]{1,0:T(8,128)(2,1)} %bitcast.14, bf16[8,128]{1,0:T(8,128)(2,1)} %refs_5_.1, ...), custom_call_target="tpu_custom_call" | custom-call | flops 2000000000 | bytes 2000000 | tf_op jit(solution)/shard_map/pallas_call | solution.py:561
  21.9 1.6 %shard_map.176 = (bf16[512,128]{1,0:T(8,128)(2,1)}, f32[16,32]{1,0:T(8,128)}, f32[32,32]{1,0:T(8,128)}) custom-call(bf16[512,128]{1,0:T(8,128)(2,1)} %get-tuple-element.9.feat_in, f32[16,32]{1,0:T(8,128)} %get-tuple-element.10.energy_in, f32[32,32]{1,0:T(8,128)} %get-tuple-element.11.forces_in), custom_call_target="tpu_custom_call" | custom-call | tf_op jit(solution)/shard_map/pallas_call | solution.py:600
